TPU v7x, 256 devices: a whole 4x4x8 slice. The times are simulated.
256 devices in a mesh: img: 32 (over z, x), txt: 8 (over y, core).
Axes of the slice: x: 4, y: 4, z: 8, core: 2. Of those that a mesh axis runs over, the one named last changes fastest.
Arguments:
- image_pooled: bfloat16 [16384, 1664], P('img', 'txt'), may hold values from -6 to 6
- text_pooled: bfloat16 [16384, 1280], P('txt', 'img'), may hold values from -6 to 6
- image_proj: bfloat16 [1664, 1280], P('txt'), may hold values from -1.5 to 1.5
- text_proj: bfloat16 [1280, 1280], P('img'), may hold values from -2 to 2
- teacher_scale: float32 [1], replicated, may hold values from 280 to 400
Outputs:
- image_targets: float32 [16384, 16384], P('img', 'txt')
- text_targets: float32 [16384, 16384], P('img', 'txt')
All inputs are finite; a program needn't handle non-finite values.
Results may differ from a plain program's by a relative error of at most 0.0011.
Values may be sent and summed in bfloat16 or wider, within the bound.
No kernel may reach another device: no remote copies, remote signals or barrier semaphores. Data moves between devices by JAX's collectives and lax.ppermute only.
A program may use at most 64 MiB of HBM per device.

v0:
```python
import functools
import math

import jax
import jax.numpy as jnp
from jax import lax
from jax.experimental import pallas as pl
from jax.experimental.pallas import tpu as pltpu
from jax.sharding import Mesh, PartitionSpec as P

SIZES = {"z": 8, "x": 4, "y": 4, "core": 2}
IMG = ("z", "x")
TXT = ("y", "core")
ROWS_A = 512
TILE = 512
VMEM_LIMIT = 24 * 1024 * 1024
BUSY = pl.CostEstimate(flops=10**10, bytes_accessed=10**7, transcendentals=0)


def shift(value, axis, step):
    count = SIZES[axis]
    return lax.ppermute(value, axis, [(i, (i + step) % count) for i in range(count)])


def after(value, *others):
    return lax.optimization_barrier((value, *others))[0]


def together(*values):
    return lax.optimization_barrier(values)


def params():
    return pltpu.CompilerParams(vmem_limit_bytes=VMEM_LIMIT)


def whole():
    return pl.BlockSpec(memory_space=pltpu.VMEM)


def fixed(*shape):
    return pl.BlockSpec(shape, lambda j: (0,) * len(shape), pipeline_mode=pl.Buffered(1))


def from_hbm(values):
    return [pltpu.with_memory_space_constraint(value, pltpu.HBM) for value in values]


def anywhere(count):
    return [pl.BlockSpec(memory_space=pl.ANY)] * count


def fetch(pairs, sem):
    copies = [pltpu.make_async_copy(source, target, sem.at[i]) for i, (source, target) in enumerate(pairs)]
    for copy in copies:
        copy.start()
    return copies


def join_kernel(*refs):
    *blocks, joined, lines, sem = refs
    depth = blocks[0].shape[0]
    copies = fetch([(block, lines.at[i]) for i, block in enumerate(blocks)], sem)
    for i, copy in enumerate(copies):
        copy.wait()
        joined[i * depth : (i + 1) * depth, :] = lines[i]


def join(blocks):
    depth, width = blocks[0].shape
    return pl.pallas_call(
        join_kernel,
        out_shape=jax.ShapeDtypeStruct((len(blocks) * depth, width), jnp.bfloat16),
        in_specs=anywhere(len(blocks)),
        out_specs=whole(),
        scratch_shapes=[
            pltpu.VMEM((len(blocks), depth, width), jnp.bfloat16),
            pltpu.SemaphoreType.DMA((len(blocks),)),
        ],
        compiler_params=params(),
        name="join",
    )(*from_hbm(blocks))


def in_turn(own, ahead, back):
    order = [own]
    for pair in zip(ahead, back):
        order += pair
    return order


def place(chunk, position, depth, features, weight):
    for i in range(4):
        at, to = i * depth, (i * 8 + position) * depth
        features[to : to + depth, :] = chunk[at : at + depth, :ROWS_A]
        weight[to : to + depth, :] = chunk[at : at + depth, ROWS_A:]


def split_kernel(depth, *refs):
    *chunks, features, weight, lines, sem = refs
    copies = fetch([(chunk, lines.at[i]) for i, chunk in enumerate(chunks)], sem)
    for i, copy in enumerate(copies):
        copy.wait()
        place(lines.at[i], i, depth, features, weight)


def split_chunks(chunks, depth):
    width = chunks[0].shape[1]
    return pl.pallas_call(
        functools.partial(split_kernel, depth),
        out_shape=(
            jax.ShapeDtypeStruct((32 * depth, ROWS_A), jnp.bfloat16),
            jax.ShapeDtypeStruct((32 * depth, width - ROWS_A), jnp.bfloat16),
        ),
        in_specs=anywhere(len(chunks)),
        out_specs=(whole(), whole()),
        scratch_shapes=[
            pltpu.VMEM((len(chunks), 4 * depth, width), jnp.bfloat16),
            pltpu.SemaphoreType.DMA((len(chunks),)),
        ],
        compiler_params=params(),
        name="split_chunks",
        cost_estimate=BUSY,
    )(*from_hbm(chunks))


def image_kernel(rows, own, other, unit):
    total = None
    for lines in (own, other):
        part = lax.dot_general(
            lines[:, :rows],
            lines[:, rows:],
            (((0,), (0,)), ((), ())),
            preferred_element_type=jnp.float32,
        )
        total = part if total is None else total + part
    count = total.shape[1]
    mean = jnp.sum(total * total, axis=1, keepdims=True) / count
    unit[...] = (total * (lax.rsqrt(mean + 1e-06) / math.sqrt(count))).astype(jnp.bfloat16)


def image_units(rows, own, other):
    return pl.pallas_call(
        functools.partial(image_kernel, rows),
        out_shape=jax.ShapeDtypeStruct((rows, own.shape[1] - rows), jnp.bfloat16),
        grid=(1,),
        in_specs=[fixed(*own.shape), fixed(*own.shape)],
        out_specs=fixed(rows, own.shape[1] - rows),
        compiler_params=params(),
        name="image_units",
        cost_estimate=BUSY,
    )(own, other)


def lanes(value):
    return [value[:, at : at + 128] for at in range(0, value.shape[1], 128)]


def score_tile(scale, weight, image, features, logits, col_part, top, total):
    text_sum = jnp.dot(weight, features, preferred_element_type=jnp.float32)
    count = text_sum.shape[0]
    mean = jnp.sum(text_sum * text_sum, axis=0, keepdims=True) / count
    unit = (text_sum * (lax.rsqrt(mean + 1e-06) / math.sqrt(count))).astype(jnp.bfloat16)
    block = scale[0] * jnp.dot(image, unit, preferred_element_type=jnp.float32)
    logits[...] = block
    col_top = jnp.max(block, axis=0, keepdims=True)
    col_part[...] = col_top + jnp.log(jnp.sum(jnp.exp(block - col_top), axis=0, keepdims=True))
    groups = lanes(block)
    old_top = top[...]
    new_top = functools.reduce(jnp.maximum, groups, old_top)
    fresh = sum(jnp.exp(group - new_top) for group in groups)
    total[...] = total[...] * jnp.exp(old_top - new_top) + fresh
    top[...] = new_top


def tiles_of(text):
    columns = text.shape[1]
    return [(text, at, min(TILE, columns - at)) for at in range(0, columns, TILE)]


def score_kernel(depth, core, scale, own, other, far_own, far_other, image, text_a, *refs):
    chunks_b, (logits, col_part, row_part, *scratch) = refs[:5], refs[5:]
    own_in, other_in, far_in, image_in, a_in, b_in, weight, logits_in, top, total, sem = scratch
    pairs = [(own, own_in), (far_own, far_in.at[0]), (other, other_in), (far_other, far_in.at[1])]
    pairs += [(text_a, a_in), (image, image_in)]
    at = 0
    for chunk in chunks_b:
        pairs.append((chunk, b_in.at[pl.ds(at, chunk.shape[0]), :]))
        at += chunk.shape[0]
    arriving = fetch(pairs, sem)
    top[...] = jnp.full_like(top, -1e30)
    total[...] = jnp.zeros_like(total)
    half = own.shape[1]
    for copy in arriving[:2]:
        copy.wait()
    arriving[4].wait()
    place(far_in.at[0], 7, depth, a_in, own_in)
    weight[pl.ds(pl.multiple_of(core[0] * half, half), half), :] = own_in[...].T
    for copy in arriving[2:4]:
        copy.wait()
    for i in range(4):
        at, to = i * depth, (i * 8 + 7) * depth
        other_in[to : to + depth, :] = far_in[1, at : at + depth, ROWS_A:]
    weight[pl.ds(pl.multiple_of((1 - core[0]) * half, half), half), :] = other_in[...].T
    arriving[5].wait()
    tiles = tiles_of(a_in) + tiles_of(b_in)
    leaving, to = [], 0
    for i, (text, at, count) in enumerate(tiles):
        if text is b_in and at == 0:
            for copy in arriving[6:]:
                copy.wait()
        here = pl.ds(to, count)
        block = logits_in.at[:, here]
        score_tile(
            scale, weight[...], image_in[...], text[:, pl.ds(at, count)], block, col_part.at[:, here], top, total
        )
        leaving.append(pltpu.make_async_copy(block, logits.at[:, here], sem.at[len(pairs) + i]))
        leaving[-1].start()
        to += count
    row_top = jnp.max(top[...], axis=1, keepdims=True)
    row_sum = jnp.sum(total[...] * jnp.exp(top[...] - row_top), axis=1, keepdims=True)
    row_part[...] = row_top + jnp.log(row_sum)
    for copy in leaving:
        copy.wait()


def score(depth, core, scale, own, other, far_own, far_other, image, text_a, chunks_b):
    rows, count = image.shape
    width_a, width_b = text_a.shape[1], chunks_b[0].shape[1]
    columns = width_a + width_b
    smem = pl.BlockSpec(memory_space=pltpu.SMEM)
    values = [own, other, far_own, far_other, image, text_a, *chunks_b]
    return pl.pallas_call(
        functools.partial(score_kernel, depth),
        out_shape=(
            pltpu.HBM((rows, columns), jnp.float32),
            jax.ShapeDtypeStruct((1, columns), jnp.float32),
            jax.ShapeDtypeStruct((rows, 1), jnp.float32),
        ),
        in_specs=[smem, smem] + anywhere(len(values)),
        out_specs=(pl.BlockSpec(memory_space=pltpu.HBM), whole(), whole()),
        scratch_shapes=[
            pltpu.VMEM(own.shape, jnp.bfloat16),
            pltpu.VMEM(own.shape, jnp.bfloat16),
            pltpu.VMEM((2, *far_own.shape), jnp.bfloat16),
            pltpu.VMEM(image.shape, jnp.bfloat16),
            pltpu.VMEM(text_a.shape, jnp.bfloat16),
            pltpu.VMEM((own.shape[0], width_b), jnp.bfloat16),
            pltpu.VMEM((count, own.shape[0]), jnp.bfloat16),
            pltpu.VMEM((rows, columns), jnp.float32),
            pltpu.VMEM((rows, 128), jnp.float32),
            pltpu.VMEM((rows, 128), jnp.float32),
            pltpu.SemaphoreType.DMA((len(values) + columns // TILE + 2,)),
        ],
        compiler_params=pltpu.CompilerParams(vmem_limit_bytes=44 * 1024 * 1024),
        name="score",
    )(core, scale, own, other, far_own, far_other, image, text_a, *from_hbm(chunks_b[:3]), *chunks_b[3:])


def minus_kernel(logits, lse, out, lines, sem_in, sem_out):
    count, tall, _ = lines.shape
    parts = [pl.ds(i * tall, tall) for i in range(count)]
    arriving = fetch([(logits.at[here, :], lines.at[i]) for i, here in enumerate(parts)], sem_in)
    leaving = []
    for i, here in enumerate(parts):
        arriving[i].wait()
        lines[i] = lines[i] - (lse[...] if lse.shape[0] == 1 else lse[here, :])
        leaving.append(pltpu.make_async_copy(lines.at[i], out.at[here, :], sem_out.at[i]))
        leaving[-1].start()
    for copy in leaving:
        copy.wait()


def minus(logits, lse):
    rows, columns = logits.shape
    parts = 8
    return pl.pallas_call(
        minus_kernel,
        out_shape=pltpu.HBM((rows, columns), jnp.float32),
        in_specs=[pl.BlockSpec(memory_space=pl.ANY), whole()],
        out_specs=pl.BlockSpec(memory_space=pltpu.HBM),
        scratch_shapes=[
            pltpu.VMEM((parts, rows // parts, columns), jnp.float32),
            pltpu.SemaphoreType.DMA((parts,)),
            pltpu.SemaphoreType.DMA((parts,)),
        ],
        compiler_params=params(),
        name="minus",
    )(*from_hbm([logits]), lse)


def add_exp(parts):
    top = jnp.max(parts, axis=0)
    return top + jnp.log(jnp.sum(jnp.exp(parts - top), axis=0))


def on_device(image_pooled, text_pooled, image_proj, text_proj, teacher_scale):
    core = lax.axis_index("core")
    width = text_proj.shape[1] // 2
    rows = image_pooled.shape[0]
    text_lines = text_pooled.T
    depth, columns = text_lines.shape
    own = lax.dynamic_slice_in_dim(text_proj, core * width, width, axis=1)

    block_a = jnp.concatenate([text_lines[:, :ROWS_A], own], axis=1)
    block_b = text_lines[:, ROWS_A:]
    image_lines = jnp.concatenate([image_pooled.T, image_proj], axis=1)

    ahead_b, back_b = [shift(block_b, "z", 1)], [shift(block_b, "z", -1)]
    block_a = join([block_a] + [shift(block_a, "x", step) for step in (1, -1, 2)])
    block_a, ahead_b[0], back_b[0], image_lines = together(block_a, ahead_b[0], back_b[0], image_lines)

    ahead_a, back_a = [shift(block_a, "z", 1)], [shift(block_a, "z", -1)]
    ahead_b.append(shift(ahead_b[0], "z", 1))
    back_b.append(shift(back_b[0], "z", -1))
    spread = jnp.broadcast_to(image_lines[None], (SIZES["y"],) + image_lines.shape)
    image_own = lax.all_to_all(spread, "y", 0, 0).reshape(-1, image_lines.shape[1])
    ahead_a[0], back_a[0], ahead_b[1], back_b[1] = together(ahead_a[0], back_a[0], ahead_b[1], back_b[1])

    ahead_a.append(shift(ahead_a[0], "z", 1))
    back_a.append(shift(back_a[0], "z", -1))
    ahead_b.append(shift(ahead_b[1], "z", 1))
    back_b.append(shift(back_b[1], "z", -1))
    far_b = shift(ahead_b[2], "z", 1)
    blocks_b = [after(block_b, ahead_b[0])]
    for step in range(3):
        later = ahead_b[step + 1] if step < 2 else far_b
        blocks_b += [after(ahead_b[step], later), after(back_b[step], later)]
    block_b = jnp.concatenate(blocks_b + [far_b], axis=0)
    ahead_a[1], back_a[1], block_b = together(ahead_a[1], back_a[1], block_b)

    ahead_a.append(shift(ahead_a[1], "z", 1))
    back_a.append(shift(back_a[1], "z", -1))
    ahead_x, back_x = shift(block_b, "x", 1), shift(block_b, "x", -1)
    half = block_b.shape[0] // 2
    ahead_a[2], back_a[2], from_ahead, from_back, image_own = together(
        ahead_a[2], back_a[2], ahead_x[:half], back_x[half:], image_own
    )

    far_a = shift(ahead_a[2], "z", 1)
    far_x = [shift(from_ahead, "x", 1), shift(from_back, "x", -1)]
    image_other = shift(image_own, "core", 1)
    image_unit = image_units(rows, image_own, image_other)

    text_a, weight_own = split_chunks(in_turn(block_a, ahead_a, back_a), depth)
    weight_other = shift(weight_own, "core", 1)
    far_other = shift(far_a, "core", 1)
    chunks_b = [block_b, ahead_x, back_x, *far_x]
    logits, col_part, row_part = score(
        depth, core.reshape(1), teacher_scale, weight_own, weight_other, far_a, far_other, image_unit, text_a, chunks_b
    )
    col_part = col_part.reshape(columns // 128, 128)
    spread = jnp.broadcast_to(col_part[None], (32,) + col_part.shape)
    col_lse = add_exp(lax.all_to_all(spread, IMG, 0, 0)).reshape(-1)

    row_part = row_part.reshape(rows // 128, 128)
    row_part = add_exp(jnp.stack([row_part, shift(row_part, "core", 1)]))
    row_parts = [row_part] + [shift(row_part, "y", step) for step in (1, -1, 2)]
    row_lse = add_exp(jnp.stack(row_parts)).reshape(-1)
    image_targets = minus(logits, row_lse[:, None])
    text_targets = minus(logits, col_lse[None, :])
    return (image_targets, text_targets)


def solution(mesh):
    grid = Mesh(mesh.devices.reshape(8, 4, 4, 2), ("z", "x", "y", "core"))
    placed = (P(IMG, TXT), P(TXT, IMG), P(TXT, None), P(IMG, None), P())
    return jax.shard_map(
        on_device,
        mesh=grid,
        in_specs=placed,
        out_specs=(P(IMG, TXT), P(IMG, TXT)),
        check_vma=False,
    )
```

profile of v0, /device:TPU:32, one launch (start us, length us, event | category | flops | bytes accessed | tf_op | source)
XLA Modules:
  0.0 136.8 jit_solution(5103218192738814571)
XLA Ops:
  3.1 1.7 %collective-permute-start.1 = (bf16[40,1152]{1,0:T(8,128)(2,1)S(1)}, bf16[40,1152]{1,0:T(8,128)(2,1)S(1)}, u32[]{:S(2)}, u32[]{:S(2)}) collective-permute-start(bf16[40,1152]{1,0:T(8,128)(2,1)S(1)} %pad_maximum_fusion.1.refs_0_), channel_id=1, source_target_pairs={{0,24},{8,0},{16,8},{24,16},{1,25},{9,1},{17,9},{25,17},{2,26},{10... | collective-permute-start | bytes 276488 | tf_op jit(solution)/shard_map/ppermute | solution.py:22
  4.9 1.8 %collective-permute-start.2 = (bf16[40,1152]{1,0:T(8,128)(2,1)S(1)}, bf16[40,1152]{1,0:T(8,128)(2,1)S(1)}, u32[]{:S(2)}, u32[]{:S(2)}) collective-permute-start(bf16[40,1152]{1,0:T(8,128)(2,1)S(1)} %pad_maximum_fusion.1.refs_0_), channel_id=1, source_target_pairs={{0,16},{8,24},{16,0},{24,8},{1,17},{9,25},{17,1},{25,9},{2,18},{10... | collective-permute-start | bytes 276488 | tf_op jit(solution)/shard_map/ppermute | solution.py:22
  7.6 2.0 %collective-permute-start.3 = (bf16[40,1536]{1,0:T(8,128)(2,1)S(1)}, bf16[40,1536]{1,0:T(8,128)(2,1)}, u32[]{:S(2)}, u32[]{:S(2)}) collective-permute-start(bf16[40,1536]{1,0:T(8,128)(2,1)S(1)} %slice.17), channel_id=1, source_target_pairs={{0,32},{32,64},{64,96},{96,128},{128,160},{160,192},{192,224},{224... | collective-permute-start | bytes 368648 | tf_op jit(solution)/shard_map/ppermute | solution.py:22
  14.6 3.0 %collective-permute-start.5 = (bf16[160,1152]{1,0:T(8,128)(2,1)S(1)}, bf16[160,1152]{1,0:T(8,128)(2,1)}, u32[]{:S(2)}, u32[]{:S(2)}) collective-permute-start(bf16[160,1152]{1,0:T(8,128)(2,1)S(1)} %join.1.refs_0_), channel_id=1, source_target_pairs={{0,32},{32,64},{64,96},{96,128},{128,160},{160,192},{192,224},{224... | collective-permute-start | bytes 1105928 | tf_op jit(solution)/shard_map/ppermute | solution.py:22
  17.6 3.2 %collective-permute-start.7 = (bf16[40,1536]{1,0:T(8,128)(2,1)}, bf16[40,1536]{1,0:T(8,128)(2,1)}, u32[]{:S(2)}, u32[]{:S(2)}) collective-permute-start(bf16[40,1536]{1,0:T(8,128)(2,1)} %collective-permute-done.3), channel_id=1, source_target_pairs={{0,32},{32,64},{64,96},{96,128},{128,160},{160,192},{192,224},{224... | collective-permute-start | bytes 368648 | tf_op jit(solution)/shard_map/ppermute | solution.py:22
  20.9 1.8 %broadcast_in_dim.6 = bf16[4,208,1792]{2,1,0:T(8,128)(2,1)} broadcast(bf16[208,1792]{1,0:T(8,128)(2,1)S(1)} %pad_maximum_fusion), dimensions={1,2} | broadcast | bytes 3727360 | tf_op jit(solution)/shard_map/broadcast_in_dim | solution.py:316
  22.7 4.5 %all-to-all-start = ((bf16[4,208,1792]{2,1,0:T(8,128)(2,1)}), bf16[4,208,1792]{2,1,0:T(8,128)(2,1)S(1)}, u32[]{:S(2)}, u32[]{:S(2)}) async-start(bf16[4,208,1792]{2,1,0:T(8,128)(2,1)} %broadcast_in_dim.6), calls=%async_computation | async-start | bytes 5963776 | tf_op jit(solution)/shard_map/all_to_all | solution.py:317
  31.7 2.8 %collective-permute-start.10 = (bf16[160,1152]{1,0:T(8,128)(2,1)}, bf16[160,1152]{1,0:T(8,128)(2,1)S(1)}, u32[]{:S(2)}, u32[]{:S(2)}) collective-permute-start(bf16[160,1152]{1,0:T(8,128)(2,1)} %collective-permute-done.6.refs_2_), channel_id=1, source_target_pairs={{0,224},{32,0},{64,32},{96,64},{128,96},{160,128},{192,160},{224,1... | collective-permute-start | bytes 1105928 | tf_op jit(solution)/shard_map/ppermute | solution.py:22
  36.2 2.0 %collective-permute-start.12 = (bf16[40,1536]{1,0:T(8,128)(2,1)S(1)}, bf16[40,1536]{1,0:T(8,128)(2,1)S(1)}, u32[]{:S(2)}, u32[]{:S(2)}) collective-permute-start(bf16[40,1536]{1,0:T(8,128)(2,1)S(1)} %collective-permute-done.11), channel_id=1, source_target_pairs={{0,32},{32,64},{64,96},{96,128},{128,160},{160,192},{192,224},{224... | collective-permute-start | bytes 368648 | tf_op jit(solution)/shard_map/ppermute | solution.py:22
  40.1 5.2 %collective-permute-done.12 = bf16[40,1536]{1,0:T(8,128)(2,1)S(1)} collective-permute-done((bf16[40,1536]{1,0:T(8,128)(2,1)S(1)}, bf16[40,1536]{1,0:T(8,128)(2,1)S(1)}, u32[]{:S(2)}, u32[]{:S(2)}) %collective-permute-start.12) | collective-permute-done | bytes 122912 | tf_op jit(solution)/shard_map/ppermute | solution.py:22
  46.0 2.6 %collective-permute-start.17 = (bf16[320,1536]{1,0:T(8,128)(2,1)S(1)}, bf16[320,1536]{1,0:T(8,128)(2,1)S(1)}, u32[]{:S(2)}, u32[]{:S(2)}) collective-permute-start(bf16[320,1536]{1,0:T(8,128)(2,1)S(1)} %constant_dynamic-update-slice_fusion.refs_0_), channel_id=1, source_target_pairs={{0,24},{8,0},{16,8},{24,16},{1,25},{9,1},{17,9},{25,17},{2,26},{10... | collective-permute-start | bytes 2949128 | tf_op jit(solution)/shard_map/ppermute | solution.py:22
  49.2 2.2 %collective-permute-start.15 = (bf16[160,1152]{1,0:T(8,128)(2,1)S(1)}, bf16[160,1152]{1,0:T(8,128)(2,1)}, u32[]{:S(2)}, u32[]{:S(2)}) collective-permute-start(bf16[160,1152]{1,0:T(8,128)(2,1)S(1)} %collective-permute-done.10.refs_4_), channel_id=1, source_target_pairs={{0,224},{32,0},{64,32},{96,64},{128,96},{160,128},{192,160},{224,1... | collective-permute-start | bytes 1105928 | tf_op jit(solution)/shard_map/ppermute | solution.py:22
  51.4 15.4 %collective-permute-done.16.refs_1_ = bf16[320,1536]{1,0:T(8,128)(2,1)S(1)} collective-permute-done((bf16[320,1536]{1,0:T(8,128)(2,1)S(1)}, bf16[320,1536]{1,0:T(8,128)(2,1)S(1)}, u32[]{:S(2)}, u32[]{:S(2)}) %collective-permute-start.16) | collective-permute-done | bytes 983072 | tf_op jit(solution)/shard_map/ppermute | solution.py:22
  69.7 1.8 %split_chunks.1 = (bf16[1280,512]{1,0:T(8,128)(2,1)S(1)}, bf16[1280,640]{1,0:T(8,128)(2,1)S(1)}) custom-call(bf16[160,1152]{1,0:T(8,128)(2,1)} %copy-done.1, bf16[160,1152]{1,0:T(8,128)(2,1)} %collective-permute-done.5.refs_1_, bf16[160,1152]{1,0:T(8,128)(2,1)} %collective-permute-done.6.refs_2_, bf16[160,1152]{1,0:T(8,128)(2,1)} %copy-done.13, ...), custom_call_target="tpu_custom_call" | custom-call | flops 10000000000 | bytes 10000000 | tf_op jit(solution)/shard_map/split_chunks/pallas_call | solution.py:109
  74.0 3.2 %collective-permute-start.23 = (bf16[160,1536]{1,0:T(8,128)(2,1)S(1)}, bf16[160,1536]{1,0:T(8,128)(2,1)S(1)}, u32[]{:S(2)}, u32[]{:S(2)}) collective-permute-start(bf16[160,1536]{1,0:T(8,128)(2,1)S(1)} %copy-done.6), channel_id=1, source_target_pairs={{0,24},{8,0},{16,8},{24,16},{1,25},{9,1},{17,9},{25,17},{2,26},{10... | collective-permute-start | bytes 1474568 | tf_op jit(solution)/shard_map/ppermute | solution.py:22
  77.2 6.9 %collective-permute-done.19.far_own = bf16[160,1152]{1,0:T(8,128)(2,1)S(1)} collective-permute-done((bf16[160,1152]{1,0:T(8,128)(2,1)S(1)}, bf16[160,1152]{1,0:T(8,128)(2,1)S(1)}, u32[]{:S(2)}, u32[]{:S(2)}) %collective-permute-start.19) | collective-permute-done | bytes 368672 | tf_op jit(solution)/shard_map/ppermute | solution.py:22
  84.1 3.1 %image_units.1.image = bf16[512,1280]{1,0:T(8,128)(2,1)S(1)} custom-call(bf16[832,1792]{1,0:T(8,128)(2,1)S(1)} %bitcast.18, bf16[832,1792]{1,0:T(8,128)(2,1)S(1)} %collective-permute-done.21.other), custom_call_target="tpu_custom_call" | custom-call | flops 10000000000 | bytes 10000000 | tf_op jit(solution)/shard_map/image_units/pallas_call | solution.py:143
  88.1 15.3 %score.1 = (f32[512,2048]{1,0:T(8,128)}, f32[1,2048]{1,0:T(1,128)S(1)}, f32[512,1]{1,0:T(8,128)S(1)}) custom-call(s32[1]{0:T(128)} %bitcast.core, f32[1]{0:T(128)S(6)} %copy.16.scale, bf16[1280,640]{1,0:T(8,128)(2,1)S(1)} %get-tuple-element.50.own, bf16[1280,640]{1,0:T(8,128)(2,1)S(1)} %collective-permute-done.18.other, ...), custom_call_target="tpu_custom_call" | custom-call | tf_op jit(solution)/shard_map/score/pallas_call | solution.py:233
  106.7 1.7 %collective-permute-start.26 = (f32[4,128]{1,0:T(4,128)S(1)}, f32[4,128]{1,0:T(4,128)S(1)}, u32[]{:S(2)}, u32[]{:S(2)}) collective-permute-start(f32[4,128]{1,0:T(4,128)S(1)} %log_add_fusion.2), channel_id=1, source_target_pairs={{0,6},{2,0},{4,2},{6,4},{1,7},{3,1},{5,3},{7,5},{8,14},{10,8},{12,... | collective-permute-start | bytes 6152 | tf_op jit(solution)/shard_map/ppermute | solution.py:22
  108.4 1.8 %collective-permute-start.27 = (f32[4,128]{1,0:T(4,128)S(1)}, f32[4,128]{1,0:T(4,128)S(1)}, u32[]{:S(2)}, u32[]{:S(2)}) collective-permute-start(f32[4,128]{1,0:T(4,128)S(1)} %log_add_fusion.2), channel_id=1, source_target_pairs={{0,4},{2,6},{4,0},{6,2},{1,5},{3,7},{5,1},{7,3},{8,12},{10,14},{12... | collective-permute-start | bytes 6152 | tf_op jit(solution)/shard_map/ppermute | solution.py:22
  110.9 10.4 %all-to-all-start.1 = ((f32[32,16,128]{2,1,0:T(8,128)}), f32[32,16,128]{2,1,0:T(8,128)S(1)}, u32[]{:S(2)}, u32[]{:S(2)}) async-start(f32[32,16,128]{2,1,0:T(8,128)} %broadcast_in_dim.8), calls=%async_computation.1 | async-start | bytes 524288 | tf_op jit(solution)/shard_map/all_to_all | solution.py:354
  121.6 3.4 %minus.2 = f32[512,2048]{1,0:T(8,128)} custom-call(f32[512,2048]{1,0:T(8,128)} %get-tuple-element.55.logits, f32[512,1]{1,0:T(8,128)S(1)} %copy.8.lse), custom_call_target="tpu_custom_call" | custom-call | tf_op jit(solution)/shard_map/minus/pallas_call | solution.py:277
  125.0 7.9 %all-to-all-done.1 = f32[32,16,128]{2,1,0:T(8,128)S(1)} async-done(((f32[32,16,128]{2,1,0:T(8,128)}), f32[32,16,128]{2,1,0:T(8,128)S(1)}, u32[]{:S(2)}, u32[]{:S(2)}) %all-to-all-start.1) | async-done | bytes 262176 | tf_op jit(solution)/shard_map/all_to_all | solution.py:354
  133.1 3.5 %minus.3 = f32[512,2048]{1,0:T(8,128)} custom-call(f32[512,2048]{1,0:T(8,128)} %get-tuple-element.55.logits, f32[1,2048]{1,0:T(1,128)S(1)} %bitcast.19), custom_call_target="tpu_custom_call" | custom-call | tf_op jit(solution)/shard_map/minus/pallas_call | solution.py:277
  (102 shorter events, 27.5 us)
Async XLA Ops:
  1.6 9.3 %collective-permute-start = (bf16[40,1152]{1,0:T(8,128)(2,1)S(1)}, bf16[40,1152]{1,0:T(8,128)(2,1)S(1)}, u32[]{:S(2)}, u32[]{:S(2)}) collective-permute-start(bf16[40,1152]{1,0:T(8,128)(2,1)S(1)} %pad_maximum_fusion.1.refs_0_), channel_id=1, source_target_pairs={{0,8},{8,16},{16,24},{24,0},{1,9},{9,17},{17,25},{25,1},{2,10},{10... | collective-permute-start | bytes 276488 | tf_op jit(solution)/shard_map/ppermute | solution.py:22
  3.1 7.7 %collective-permute-start.1 = (bf16[40,1152]{1,0:T(8,128)(2,1)S(1)}, bf16[40,1152]{1,0:T(8,128)(2,1)S(1)}, u32[]{:S(2)}, u32[]{:S(2)}) collective-permute-start(bf16[40,1152]{1,0:T(8,128)(2,1)S(1)} %pad_maximum_fusion.1.refs_0_), channel_id=1, source_target_pairs={{0,24},{8,0},{16,8},{24,16},{1,25},{9,1},{17,9},{25,17},{2,26},{10... | collective-permute-start | bytes 276488 | tf_op jit(solution)/shard_map/ppermute | solution.py:22
  14.6 15.0 %collective-permute-start.5 = (bf16[160,1152]{1,0:T(8,128)(2,1)S(1)}, bf16[160,1152]{1,0:T(8,128)(2,1)}, u32[]{:S(2)}, u32[]{:S(2)}) collective-permute-start(bf16[160,1152]{1,0:T(8,128)(2,1)S(1)} %join.1.refs_0_), channel_id=1, source_target_pairs={{0,32},{32,64},{64,96},{96,128},{128,160},{160,192},{192,224},{224... | collective-permute-start | bytes 1105928 | tf_op jit(solution)/shard_map/ppermute | solution.py:22
  17.6 12.0 %collective-permute-start.6 = (bf16[160,1152]{1,0:T(8,128)(2,1)S(1)}, bf16[160,1152]{1,0:T(8,128)(2,1)}, u32[]{:S(2)}, u32[]{:S(2)}) collective-permute-start(bf16[160,1152]{1,0:T(8,128)(2,1)S(1)} %join.1.refs_0_), channel_id=1, source_target_pairs={{0,224},{32,0},{64,32},{96,64},{128,96},{160,128},{192,160},{224,1... | collective-permute-start | bytes 1105928 | tf_op jit(solution)/shard_map/ppermute | solution.py:22
  17.6 10.4 %collective-permute-start.7 = (bf16[40,1536]{1,0:T(8,128)(2,1)}, bf16[40,1536]{1,0:T(8,128)(2,1)}, u32[]{:S(2)}, u32[]{:S(2)}) collective-permute-start(bf16[40,1536]{1,0:T(8,128)(2,1)} %collective-permute-done.3), channel_id=1, source_target_pairs={{0,32},{32,64},{64,96},{96,128},{128,160},{160,192},{192,224},{224... | collective-permute-start | bytes 368648 | tf_op jit(solution)/shard_map/ppermute | solution.py:22
  20.9 8.8 %collective-permute-start.8 = (bf16[40,1536]{1,0:T(8,128)(2,1)}, bf16[40,1536]{1,0:T(8,128)(2,1)}, u32[]{:S(2)}, u32[]{:S(2)}) collective-permute-start(bf16[40,1536]{1,0:T(8,128)(2,1)} %collective-permute-done.4), channel_id=1, source_target_pairs={{0,224},{32,0},{64,32},{96,64},{128,96},{160,128},{192,160},{224,1... | collective-permute-start | bytes 368648 | tf_op jit(solution)/shard_map/ppermute | solution.py:22
  22.7 46.9 %all-to-all-start = ((bf16[4,208,1792]{2,1,0:T(8,128)(2,1)}), bf16[4,208,1792]{2,1,0:T(8,128)(2,1)S(1)}, u32[]{:S(2)}, u32[]{:S(2)}) async-start(bf16[4,208,1792]{2,1,0:T(8,128)(2,1)} %broadcast_in_dim.6), calls=%async_computation | async-start | bytes 5963776 | tf_op jit(solution)/shard_map/all_to_all | solution.py:317
  31.4 13.9 %collective-permute-start.13 = (bf16[40,1536]{1,0:T(8,128)(2,1)}, bf16[40,1536]{1,0:T(8,128)(2,1)S(1)}, u32[]{:S(2)}, u32[]{:S(2)}) collective-permute-start(bf16[40,1536]{1,0:T(8,128)(2,1)} %collective-permute-done.8), channel_id=1, source_target_pairs={{0,224},{32,0},{64,32},{96,64},{128,96},{160,128},{192,160},{224,1... | collective-permute-start | bytes 368648 | tf_op jit(solution)/shard_map/ppermute | solution.py:22
  31.7 13.7 %collective-permute-start.10 = (bf16[160,1152]{1,0:T(8,128)(2,1)}, bf16[160,1152]{1,0:T(8,128)(2,1)S(1)}, u32[]{:S(2)}, u32[]{:S(2)}) collective-permute-start(bf16[160,1152]{1,0:T(8,128)(2,1)} %collective-permute-done.6.refs_2_), channel_id=1, source_target_pairs={{0,224},{32,0},{64,32},{96,64},{128,96},{160,128},{192,160},{224,1... | collective-permute-start | bytes 1105928 | tf_op jit(solution)/shard_map/ppermute | solution.py:22
  34.4 10.9 %collective-permute-start.9 = (bf16[160,1152]{1,0:T(8,128)(2,1)}, bf16[160,1152]{1,0:T(8,128)(2,1)S(1)}, u32[]{:S(2)}, u32[]{:S(2)}) collective-permute-start(bf16[160,1152]{1,0:T(8,128)(2,1)} %collective-permute-done.5.refs_1_), channel_id=1, source_target_pairs={{0,32},{32,64},{64,96},{96,128},{128,160},{160,192},{192,224},{224... | collective-permute-start | bytes 1105928 | tf_op jit(solution)/shard_map/ppermute | solution.py:22
  36.2 9.0 %collective-permute-start.12 = (bf16[40,1536]{1,0:T(8,128)(2,1)S(1)}, bf16[40,1536]{1,0:T(8,128)(2,1)S(1)}, u32[]{:S(2)}, u32[]{:S(2)}) collective-permute-start(bf16[40,1536]{1,0:T(8,128)(2,1)S(1)} %collective-permute-done.11), channel_id=1, source_target_pairs={{0,32},{32,64},{64,96},{96,128},{128,160},{160,192},{192,224},{224... | collective-permute-start | bytes 368648 | tf_op jit(solution)/shard_map/ppermute | solution.py:22
  45.4 21.5 %collective-permute-start.16 = (bf16[320,1536]{1,0:T(8,128)(2,1)S(1)}, bf16[320,1536]{1,0:T(8,128)(2,1)S(1)}, u32[]{:S(2)}, u32[]{:S(2)}) collective-permute-start(bf16[320,1536]{1,0:T(8,128)(2,1)S(1)} %constant_dynamic-update-slice_fusion.refs_0_), channel_id=1, source_target_pairs={{0,8},{8,16},{16,24},{24,0},{1,9},{9,17},{17,25},{25,1},{2,10},{10... | collective-permute-start | bytes 2949128 | tf_op jit(solution)/shard_map/ppermute | solution.py:22
  46.0 21.7 %collective-permute-start.17 = (bf16[320,1536]{1,0:T(8,128)(2,1)S(1)}, bf16[320,1536]{1,0:T(8,128)(2,1)S(1)}, u32[]{:S(2)}, u32[]{:S(2)}) collective-permute-start(bf16[320,1536]{1,0:T(8,128)(2,1)S(1)} %constant_dynamic-update-slice_fusion.refs_0_), channel_id=1, source_target_pairs={{0,24},{8,0},{16,8},{24,16},{1,25},{9,1},{17,9},{25,17},{2,26},{10... | collective-permute-start | bytes 2949128 | tf_op jit(solution)/shard_map/ppermute | solution.py:22
  48.7 20.0 %collective-permute-start.14 = (bf16[160,1152]{1,0:T(8,128)(2,1)S(1)}, bf16[160,1152]{1,0:T(8,128)(2,1)S(1)}, u32[]{:S(2)}, u32[]{:S(2)}) collective-permute-start(bf16[160,1152]{1,0:T(8,128)(2,1)S(1)} %collective-permute-done.9.refs_3_), channel_id=1, source_target_pairs={{0,32},{32,64},{64,96},{96,128},{128,160},{160,192},{192,224},{224... | collective-permute-start | bytes 1105928 | tf_op jit(solution)/shard_map/ppermute | solution.py:22
  49.2 20.4 %collective-permute-start.15 = (bf16[160,1152]{1,0:T(8,128)(2,1)S(1)}, bf16[160,1152]{1,0:T(8,128)(2,1)}, u32[]{:S(2)}, u32[]{:S(2)}) collective-permute-start(bf16[160,1152]{1,0:T(8,128)(2,1)S(1)} %collective-permute-done.10.refs_4_), channel_id=1, source_target_pairs={{0,224},{32,0},{64,32},{96,64},{128,96},{160,128},{192,160},{224,1... | collective-permute-start | bytes 1105928 | tf_op jit(solution)/shard_map/ppermute | solution.py:22
  69.6 14.5 %collective-permute-start.21 = (bf16[832,1792]{1,0:T(8,128)(2,1)S(1)}, bf16[832,1792]{1,0:T(8,128)(2,1)S(1)}, u32[]{:S(2)}, u32[]{:S(2)}) collective-permute-start(bf16[832,1792]{1,0:T(8,128)(2,1)S(1)} %bitcast.17), channel_id=1, source_target_pairs={{0,1},{1,0},{2,3},{3,2},{4,5},{5,4},{6,7},{7,6},{8,9},{9,8},{10,11... | collective-permute-start | bytes 8945672 | tf_op jit(solution)/shard_map/ppermute | solution.py:22
  71.6 16.6 %collective-permute-start.18 = (bf16[1280,640]{1,0:T(8,128)(2,1)S(1)}, bf16[1280,640]{1,0:T(8,128)(2,1)S(1)}, u32[]{:S(2)}, u32[]{:S(2)}) collective-permute-start(bf16[1280,640]{1,0:T(8,128)(2,1)S(1)} %get-tuple-element.50.own), channel_id=1, source_target_pairs={{0,1},{1,0},{2,3},{3,2},{4,5},{5,4},{6,7},{7,6},{8,9},{9,8},{10,11... | collective-permute-start | bytes 4915208 | tf_op jit(solution)/shard_map/ppermute | solution.py:22
  72.1 12.0 %collective-permute-start.19 = (bf16[160,1152]{1,0:T(8,128)(2,1)S(1)}, bf16[160,1152]{1,0:T(8,128)(2,1)S(1)}, u32[]{:S(2)}, u32[]{:S(2)}) collective-permute-start(bf16[160,1152]{1,0:T(8,128)(2,1)S(1)} %copy-done.15), channel_id=1, source_target_pairs={{0,32},{32,64},{64,96},{96,128},{128,160},{160,192},{192,224},{224... | collective-permute-start | bytes 1105928 | tf_op jit(solution)/shard_map/ppermute | solution.py:22
  73.9 14.2 %collective-permute-start.22 = (bf16[160,1536]{1,0:T(8,128)(2,1)S(1)}, bf16[160,1536]{1,0:T(8,128)(2,1)S(1)}, u32[]{:S(2)}, u32[]{:S(2)}) collective-permute-start(bf16[160,1536]{1,0:T(8,128)(2,1)S(1)} %copy-done.5), channel_id=1, source_target_pairs={{0,8},{8,16},{16,24},{24,0},{1,9},{9,17},{17,25},{25,1},{2,10},{10... | collective-permute-start | bytes 1474568 | tf_op jit(solution)/shard_map/ppermute | solution.py:22
  74.0 14.1 %collective-permute-start.23 = (bf16[160,1536]{1,0:T(8,128)(2,1)S(1)}, bf16[160,1536]{1,0:T(8,128)(2,1)S(1)}, u32[]{:S(2)}, u32[]{:S(2)}) collective-permute-start(bf16[160,1536]{1,0:T(8,128)(2,1)S(1)} %copy-done.6), channel_id=1, source_target_pairs={{0,24},{8,0},{16,8},{24,16},{1,25},{9,1},{17,9},{25,17},{2,26},{10... | collective-permute-start | bytes 1474568 | tf_op jit(solution)/shard_map/ppermute | solution.py:22
  105.1 16.2 %collective-permute-start.25 = (f32[4,128]{1,0:T(4,128)S(1)}, f32[4,128]{1,0:T(4,128)S(1)}, u32[]{:S(2)}, u32[]{:S(2)}) collective-permute-start(f32[4,128]{1,0:T(4,128)S(1)} %log_add_fusion.2), channel_id=1, source_target_pairs={{0,2},{2,4},{4,6},{6,0},{1,3},{3,5},{5,7},{7,1},{8,10},{10,12},{12... | collective-permute-start | bytes 6152 | tf_op jit(solution)/shard_map/ppermute | solution.py:22
  106.7 14.7 %collective-permute-start.26 = (f32[4,128]{1,0:T(4,128)S(1)}, f32[4,128]{1,0:T(4,128)S(1)}, u32[]{:S(2)}, u32[]{:S(2)}) collective-permute-start(f32[4,128]{1,0:T(4,128)S(1)} %log_add_fusion.2), channel_id=1, source_target_pairs={{0,6},{2,0},{4,2},{6,4},{1,7},{3,1},{5,3},{7,5},{8,14},{10,8},{12,... | collective-permute-start | bytes 6152 | tf_op jit(solution)/shard_map/ppermute | solution.py:22
  108.4 12.9 %collective-permute-start.27 = (f32[4,128]{1,0:T(4,128)S(1)}, f32[4,128]{1,0:T(4,128)S(1)}, u32[]{:S(2)}, u32[]{:S(2)}) collective-permute-start(f32[4,128]{1,0:T(4,128)S(1)} %log_add_fusion.2), channel_id=1, source_target_pairs={{0,4},{2,6},{4,0},{6,2},{1,5},{3,7},{5,1},{7,3},{8,12},{10,14},{12... | collective-permute-start | bytes 6152 | tf_op jit(solution)/shard_map/ppermute | solution.py:22
  110.9 22.0 %all-to-all-start.1 = ((f32[32,16,128]{2,1,0:T(8,128)}), f32[32,16,128]{2,1,0:T(8,128)S(1)}, u32[]{:S(2)}, u32[]{:S(2)}) async-start(f32[32,16,128]{2,1,0:T(8,128)} %broadcast_in_dim.8), calls=%async_computation.1 | async-start | bytes 524288 | tf_op jit(solution)/shard_map/all_to_all | solution.py:354
  (22 other events, 143.2 us)
where the time goes:
time: 137 us
  starting transfers between devices  51.7 us (38%)
  waiting for transfers between devices  40.5 us (30%)
  Pallas kernels  28.2 us (21%)
  local copies, waits for them, and re-layouts  13 us (9%)
  between operations  1.86 us (1%)
  other arithmetic  1.46 us (1%)
    ppermute x28, starting transfers between devices, shift(): lax.ppermute(value, axis, [(i, (i + step) % count) for i in range(count)])  36.9 us
    ppermute x28, waiting for transfers between devices, shift(): lax.ppermute(value, axis, [(i, (i + step) % count) for i in range(count)])  32.5 us
    pallas_call x1, Pallas kernels, score(): pl.pallas_call(functools.partial(score_kernel, depth), out_shape=(pltpu.H...  15.3 us
    all_to_all x1, starting transfers between devices, on_device(): col_lse = add_exp(lax.all_to_all(spread, IMG, 0, 0)).reshape(-1)  10.4 us
    all_to_all x1, waiting for transfers between devices, on_device(): col_lse = add_exp(lax.all_to_all(spread, IMG, 0, 0)).reshape(-1)  7.93 us
    pallas_call x2, Pallas kernels, minus(): pl.pallas_call(minus_kernel, out_shape=pltpu.HBM((rows, columns), jnp.flo...  6.95 us
    unnamed x39, local copies, waits for them, and re-layouts  6.89 us
    all_to_all x1, starting transfers between devices, on_device(): lax.all_to_all(spread, 'y', 0, 0).reshape(-1, image_lines.shape[1])  4.46 us
  transfers between devices with their start and end apart: 30, of which 8 were waited for; matrix products, arithmetic and copies ran while one was open for 8% of the time, Pallas kernels for 7%

commit v1 on v0

--- a/solution.py
+++ b/solution.py
@@ -179,14 +179,12 @@
 
 
 def score_kernel(depth, core, scale, own, other, far_own, far_other, image, text_a, *refs):
-    chunks_b, (logits, col_part, row_part, *scratch) = refs[:5], refs[5:]
-    own_in, other_in, far_in, image_in, a_in, b_in, weight, logits_in, top, total, sem = scratch
+    low, high, (logits, col_part, row_part, *scratch) = refs[:4], refs[4:8], refs[8:]
+    own_in, other_in, far_in, image_in, a_in, low_in, high_in, b_in, weight, logits_in, top, total, sem = scratch
     pairs = [(own, own_in), (far_own, far_in.at[0]), (other, other_in), (far_other, far_in.at[1])]
     pairs += [(text_a, a_in), (image, image_in)]
-    at = 0
-    for chunk in chunks_b:
-        pairs.append((chunk, b_in.at[pl.ds(at, chunk.shape[0]), :]))
-        at += chunk.shape[0]
+    for i in range(4):
+        pairs += [(low[i], low_in.at[i]), (high[i], high_in.at[i])]
     arriving = fetch(pairs, sem)
     top[...] = jnp.full_like(top, -1e30)
     total[...] = jnp.zeros_like(total)
@@ -209,6 +207,10 @@
         if text is b_in and at == 0:
             for copy in arriving[6:]:
                 copy.wait()
+            cut, tall = low_in.shape[1], 8 * depth
+            for x in range(4):
+                b_in[x * tall : x * tall + cut, :] = low_in[x]
+                b_in[x * tall + cut : (x + 1) * tall, :] = high_in[x]
         here = pl.ds(to, count)
         block = logits_in.at[:, here]
         score_tile(
@@ -224,12 +226,12 @@
         copy.wait()
 
 
-def score(depth, core, scale, own, other, far_own, far_other, image, text_a, chunks_b):
+def score(depth, core, scale, own, other, far_own, far_other, image, text_a, low, high):
     rows, count = image.shape
-    width_a, width_b = text_a.shape[1], chunks_b[0].shape[1]
+    width_a, width_b = text_a.shape[1], low[0].shape[1]
     columns = width_a + width_b
     smem = pl.BlockSpec(memory_space=pltpu.SMEM)
-    values = [own, other, far_own, far_other, image, text_a, *chunks_b]
+    values = [own, other, far_own, far_other, image, text_a, *from_hbm(low[:3]), low[3], *from_hbm(high[:3]), high[3]]
     return pl.pallas_call(
         functools.partial(score_kernel, depth),
         out_shape=(
@@ -245,6 +247,8 @@
             pltpu.VMEM((2, *far_own.shape), jnp.bfloat16),
             pltpu.VMEM(image.shape, jnp.bfloat16),
             pltpu.VMEM(text_a.shape, jnp.bfloat16),
+            pltpu.VMEM((4, *low[0].shape), jnp.bfloat16),
+            pltpu.VMEM((4, *high[0].shape), jnp.bfloat16),
             pltpu.VMEM((own.shape[0], width_b), jnp.bfloat16),
             pltpu.VMEM((count, own.shape[0]), jnp.bfloat16),
             pltpu.VMEM((rows, columns), jnp.float32),
@@ -254,7 +258,7 @@
         ],
         compiler_params=pltpu.CompilerParams(vmem_limit_bytes=44 * 1024 * 1024),
         name="score",
-    )(core, scale, own, other, far_own, far_other, image, text_a, *from_hbm(chunks_b[:3]), *chunks_b[3:])
+    )(core, scale, *values)
 
 
 def minus_kernel(logits, lse, out, lines, sem_in, sem_out):
@@ -310,44 +314,57 @@
     block_a = join([block_a] + [shift(block_a, "x", step) for step in (1, -1, 2)])
     block_a, ahead_b[0], back_b[0], image_lines = together(block_a, ahead_b[0], back_b[0], image_lines)
 
+    low = jnp.concatenate([block_b, ahead_b[0], back_b[0]], axis=0)
+    ahead_low = shift(low, "x", 1)
     ahead_a, back_a = [shift(block_a, "z", 1)], [shift(block_a, "z", -1)]
     ahead_b.append(shift(ahead_b[0], "z", 1))
     back_b.append(shift(back_b[0], "z", -1))
     spread = jnp.broadcast_to(image_lines[None], (SIZES["y"],) + image_lines.shape)
     image_own = lax.all_to_all(spread, "y", 0, 0).reshape(-1, image_lines.shape[1])
-    ahead_a[0], back_a[0], ahead_b[1], back_b[1] = together(ahead_a[0], back_a[0], ahead_b[1], back_b[1])
+    ahead_a[0], back_a[0], ahead_b[1], back_b[1], ahead_low = together(
+        ahead_a[0], back_a[0], ahead_b[1], back_b[1], ahead_low
+    )
 
     ahead_a.append(shift(ahead_a[0], "z", 1))
     back_a.append(shift(back_a[0], "z", -1))
     ahead_b.append(shift(ahead_b[1], "z", 1))
     back_b.append(shift(back_b[1], "z", -1))
     far_b = shift(ahead_b[2], "z", 1)
-    blocks_b = [after(block_b, ahead_b[0])]
-    for step in range(3):
-        later = ahead_b[step + 1] if step < 2 else far_b
-        blocks_b += [after(ahead_b[step], later), after(back_b[step], later)]
-    block_b = jnp.concatenate(blocks_b + [far_b], axis=0)
-    ahead_a[1], back_a[1], block_b = together(ahead_a[1], back_a[1], block_b)
+    back_low = shift(low, "x", -1)
+    high = [after(ahead_b[1], ahead_b[2]), after(back_b[1], ahead_b[2])]
+    high += [after(ahead_b[2], far_b), after(back_b[2], far_b), far_b]
+    high = jnp.concatenate(high, axis=0)
+    ahead_a[1], back_a[1], high, back_low = together(ahead_a[1], back_a[1], high, back_low)
 
     ahead_a.append(shift(ahead_a[1], "z", 1))
     back_a.append(shift(back_a[1], "z", -1))
-    ahead_x, back_x = shift(block_b, "x", 1), shift(block_b, "x", -1)
-    half = block_b.shape[0] // 2
-    ahead_a[2], back_a[2], from_ahead, from_back, image_own = together(
-        ahead_a[2], back_a[2], ahead_x[:half], back_x[half:], image_own
+    ahead_high, back_high = shift(high, "x", 1), shift(high, "x", -1)
+    ahead_a[2], back_a[2], ahead_high, back_high, image_own = together(
+        ahead_a[2], back_a[2], ahead_high, back_high, image_own
     )
 
     far_a = shift(ahead_a[2], "z", 1)
-    far_x = [shift(from_ahead, "x", 1), shift(from_back, "x", -1)]
+    far_low, far_high = shift(ahead_low, "x", 1), shift(back_high, "x", -1)
     image_other = shift(image_own, "core", 1)
     image_unit = image_units(rows, image_own, image_other)
 
     text_a, weight_own = split_chunks(in_turn(block_a, ahead_a, back_a), depth)
     weight_other = shift(weight_own, "core", 1)
     far_other = shift(far_a, "core", 1)
-    chunks_b = [block_b, ahead_x, back_x, *far_x]
+    lows = [low, ahead_low, back_low, far_low]
+    highs = [high, ahead_high, back_high, far_high]
     logits, col_part, row_part = score(
-        depth, core.reshape(1), teacher_scale, weight_own, weight_other, far_a, far_other, image_unit, text_a, chunks_b
+        depth,
+        core.reshape(1),
+        teacher_scale,
+        weight_own,
+        weight_other,
+        far_a,
+        far_other,
+        image_unit,
+        text_a,
+        lows,
+        highs,
     )
     col_part = col_part.reshape(columns // 128, 128)
     spread = jnp.broadcast_to(col_part[None], (32,) + col_part.shape)

time: 137 us -> 134 us (0.978)
  local copies, waits for them, and re-layouts: 13 us -> 7.35 us
  starting transfers between devices: 51.7 us -> 55.3 us
  waiting for transfers between devices: 40.5 us -> 38.8 us
    ppermute x28 -> x30, starting transfers between devices: 36.9 us -> 41.9 us  [shift(): lax.ppermute(value, axis, [(i, (i + step) % count) for i in range(count)])]
    unnamed x39 -> x36, local copies, waits for them, and re-layouts: 6.89 us -> 2.94 us
    slice x2 -> x0, local copies, waits for them, and re-layouts: 1.74 us -> none  [the longest x1 0.89 us: on_device(): back_x[half:]]
    ppermute x28 -> x30, waiting for transfers between devices: 32.5 us -> 30.8 us  [shift(): lax.ppermute(value, axis, [(i, (i + step) % count) for i in range(count)])]
    all_to_all x1, starting transfers between devices: 10.4 us -> 8.95 us  [on_device(): col_lse = add_exp(lax.all_to_all(spread, IMG, 0, 0)).reshape(-1)]
  transfers between devices with their start and end apart: 30 -> 32, of which waited for: 8 -> 13; matrix products, arithmetic and copies ran while one was open for 8% -> 4% of each run, Pallas kernels for 7% -> 7%
where the time goes in v1:
time: 134 us
  starting transfers between devices  55.3 us (41%)
  waiting for transfers between devices  38.8 us (29%)
  Pallas kernels  28 us (21%)
  local copies, waits for them, and re-layouts  7.35 us (5%)
  other arithmetic  2.25 us (2%)
  between operations  1.85 us (1%)
    ppermute x30, starting transfers between devices, shift(): lax.ppermute(value, axis, [(i, (i + step) % count) for i in range(count)])  41.9 us
    ppermute x30, waiting for transfers between devices, shift(): lax.ppermute(value, axis, [(i, (i + step) % count) for i in range(count)])  30.8 us
    pallas_call x1, Pallas kernels, score(): pl.pallas_call(functools.partial(score_kernel, depth), out_shape=(pltpu.H...  15.2 us
    all_to_all x1, starting transfers between devices, on_device(): col_lse = add_exp(lax.all_to_all(spread, IMG, 0, 0)).reshape(-1)  8.95 us
    all_to_all x1, waiting for transfers between devices, on_device(): col_lse = add_exp(lax.all_to_all(spread, IMG, 0, 0)).reshape(-1)  7.93 us
    pallas_call x2, Pallas kernels, minus(): pl.pallas_call(minus_kernel, out_shape=pltpu.HBM((rows, columns), jnp.flo...  6.95 us
    all_to_all x1, starting transfers between devices, on_device(): lax.all_to_all(spread, 'y', 0, 0).reshape(-1, image_lines.shape[1])  4.46 us
    pallas_call x1, Pallas kernels, image_units(): pl.pallas_call(functools.partial(image_kernel, rows), out_shape=jax.Shape...  3.09 us
  transfers between devices with their start and end apart: 32, of which 13 were waited for; matrix products, arithmetic and copies ran while one was open for 4% of the time, Pallas kernels for 7%

profile of v1, /device:TPU:32, one launch (start us, length us, event | category | flops | bytes accessed | tf_op | source)
XLA Modules:
  0.0 133.6 jit_solution(4937750901499980767)
XLA Ops:
  15.9 3.0 %collective-permute-start.5 = (bf16[160,1152]{1,0:T(8,128)(2,1)S(1)}, bf16[160,1152]{1,0:T(8,128)(2,1)}, u32[]{:S(2)}, u32[]{:S(2)}) collective-permute-start(bf16[160,1152]{1,0:T(8,128)(2,1)S(1)} %join.1.refs_0_), channel_id=1, source_target_pairs={{0,32},{32,64},{64,96},{96,128},{128,160},{160,192},{192,224},{224... | collective-permute-start | bytes 1105928 | tf_op jit(solution)/shard_map/ppermute | solution.py:22
  20.7 4.5 %all-to-all-start = ((bf16[4,208,1792]{2,1,0:T(8,128)(2,1)}), bf16[4,208,1792]{2,1,0:T(8,128)(2,1)S(1)}, u32[]{:S(2)}, u32[]{:S(2)}) async-start(bf16[4,208,1792]{2,1,0:T(8,128)(2,1)} %broadcast_in_dim.6), calls=%async_computation | async-start | bytes 5963776 | tf_op jit(solution)/shard_map/all_to_all | solution.py:323
  25.2 3.2 %collective-permute-start.7 = (bf16[40,1536]{1,0:T(8,128)(2,1)}, bf16[40,1536]{1,0:T(8,128)(2,1)S(1)}, u32[]{:S(2)}, u32[]{:S(2)}) collective-permute-start(bf16[40,1536]{1,0:T(8,128)(2,1)} %copy-done.6), channel_id=1, source_target_pairs={{0,32},{32,64},{64,96},{96,128},{128,160},{160,192},{192,224},{224... | collective-permute-start | bytes 368648 | tf_op jit(solution)/shard_map/ppermute | solution.py:22
  28.4 2.9 %collective-permute-done.7 = bf16[40,1536]{1,0:T(8,128)(2,1)S(1)} collective-permute-done((bf16[40,1536]{1,0:T(8,128)(2,1)}, bf16[40,1536]{1,0:T(8,128)(2,1)S(1)}, u32[]{:S(2)}, u32[]{:S(2)}) %collective-permute-start.7) | collective-permute-done | bytes 122912 | tf_op jit(solution)/shard_map/ppermute | solution.py:22
  31.3 2.2 %collective-permute-done.8 = bf16[40,1536]{1,0:T(8,128)(2,1)S(1)} collective-permute-done((bf16[40,1536]{1,0:T(8,128)(2,1)}, bf16[40,1536]{1,0:T(8,128)(2,1)S(1)}, u32[]{:S(2)}, u32[]{:S(2)}) %collective-permute-start.8) | collective-permute-done | bytes 122912 | tf_op jit(solution)/shard_map/ppermute | solution.py:22
  33.5 2.1 %collective-permute-start.12 = (bf16[40,1536]{1,0:T(8,128)(2,1)S(1)}, bf16[40,1536]{1,0:T(8,128)(2,1)S(1)}, u32[]{:S(2)}, u32[]{:S(2)}) collective-permute-start(bf16[40,1536]{1,0:T(8,128)(2,1)S(1)} %collective-permute-done.7), channel_id=1, source_target_pairs={{0,32},{32,64},{64,96},{96,128},{128,160},{160,192},{192,224},{224... | collective-permute-start | bytes 368648 | tf_op jit(solution)/shard_map/ppermute | solution.py:22
  35.6 2.6 %collective-permute-start.15 = (bf16[120,1536]{1,0:T(8,128)(2,1)}, bf16[120,1536]{1,0:T(8,128)(2,1)S(1)}, u32[]{:S(2)}, u32[]{:S(2)}) collective-permute-start(bf16[120,1536]{1,0:T(8,128)(2,1)} %pad_maximum_fusion.1.refs_0_), channel_id=1, source_target_pairs={{0,24},{8,0},{16,8},{24,16},{1,25},{9,1},{17,9},{25,17},{2,26},{10... | collective-permute-start | bytes 1105928 | tf_op jit(solution)/shard_map/ppermute | solution.py:22
  38.2 3.2 %collective-permute-start.10 = (bf16[160,1152]{1,0:T(8,128)(2,1)}, bf16[160,1152]{1,0:T(8,128)(2,1)S(1)}, u32[]{:S(2)}, u32[]{:S(2)}) collective-permute-start(bf16[160,1152]{1,0:T(8,128)(2,1)} %collective-permute-done.5.refs_1_), channel_id=1, source_target_pairs={{0,32},{32,64},{64,96},{96,128},{128,160},{160,192},{192,224},{224... | collective-permute-start | bytes 1105928 | tf_op jit(solution)/shard_map/ppermute | solution.py:22
  41.5 2.0 %collective-permute-start.13 = (bf16[40,1536]{1,0:T(8,128)(2,1)S(1)}, bf16[40,1536]{1,0:T(8,128)(2,1)S(1)}, u32[]{:S(2)}, u32[]{:S(2)}) collective-permute-start(bf16[40,1536]{1,0:T(8,128)(2,1)S(1)} %collective-permute-done.12), channel_id=1, source_target_pairs={{0,32},{32,64},{64,96},{96,128},{128,160},{160,192},{192,224},{224... | collective-permute-start | bytes 368648 | tf_op jit(solution)/shard_map/ppermute | solution.py:22
  44.6 4.4 %collective-permute-done.13 = bf16[40,1536]{1,0:T(8,128)(2,1)S(1)} collective-permute-done((bf16[40,1536]{1,0:T(8,128)(2,1)S(1)}, bf16[40,1536]{1,0:T(8,128)(2,1)S(1)}, u32[]{:S(2)}, u32[]{:S(2)}) %collective-permute-start.13) | collective-permute-done | bytes 122912 | tf_op jit(solution)/shard_map/ppermute | solution.py:22
  49.2 3.2 %collective-permute-start.19 = (bf16[200,1536]{1,0:T(8,128)(2,1)S(1)}, bf16[200,1536]{1,0:T(8,128)(2,1)}, u32[]{:S(2)}, u32[]{:S(2)}) collective-permute-start(bf16[200,1536]{1,0:T(8,128)(2,1)S(1)} %constant_dynamic-update-slice_fusion.refs_4_), channel_id=1, source_target_pairs={{0,24},{8,0},{16,8},{24,16},{1,25},{9,1},{17,9},{25,17},{2,26},{10... | collective-permute-start | bytes 1843208 | tf_op jit(solution)/shard_map/ppermute | solution.py:22
  54.7 5.5 %collective-permute-done.16.refs_5_ = bf16[160,1152]{1,0:T(8,128)(2,1)S(1)} collective-permute-done((bf16[160,1152]{1,0:T(8,128)(2,1)S(1)}, bf16[160,1152]{1,0:T(8,128)(2,1)S(1)}, u32[]{:S(2)}, u32[]{:S(2)}) %collective-permute-start.16) | collective-permute-done | bytes 368672 | tf_op jit(solution)/shard_map/ppermute | solution.py:22
  60.2 2.2 %collective-permute-done.17.refs_6_ = bf16[160,1152]{1,0:T(8,128)(2,1)S(1)} collective-permute-done((bf16[160,1152]{1,0:T(8,128)(2,1)S(1)}, bf16[160,1152]{1,0:T(8,128)(2,1)S(1)}, u32[]{:S(2)}, u32[]{:S(2)}) %collective-permute-start.17) | collective-permute-done | bytes 368672 | tf_op jit(solution)/shard_map/ppermute | solution.py:22
  69.3 3.2 %collective-permute-start.25 = (bf16[200,1536]{1,0:T(8,128)(2,1)}, bf16[200,1536]{1,0:T(8,128)(2,1)S(1)}, u32[]{:S(2)}, u32[]{:S(2)}) collective-permute-start(bf16[200,1536]{1,0:T(8,128)(2,1)} %collective-permute-done.19.refs_6_), channel_id=1, source_target_pairs={{0,24},{8,0},{16,8},{24,16},{1,25},{9,1},{17,9},{25,17},{2,26},{10... | collective-permute-start | bytes 1843208 | tf_op jit(solution)/shard_map/ppermute | solution.py:22
  72.5 4.6 %collective-permute-done.21.far_own = bf16[160,1152]{1,0:T(8,128)(2,1)S(1)} collective-permute-done((bf16[160,1152]{1,0:T(8,128)(2,1)S(1)}, bf16[160,1152]{1,0:T(8,128)(2,1)S(1)}, u32[]{:S(2)}, u32[]{:S(2)}) %collective-permute-start.21) | collective-permute-done | bytes 368672 | tf_op jit(solution)/shard_map/ppermute | solution.py:22
  77.1 3.1 %image_units.1.image = bf16[512,1280]{1,0:T(8,128)(2,1)S(1)} custom-call(bf16[832,1792]{1,0:T(8,128)(2,1)S(1)} %bitcast.18, bf16[832,1792]{1,0:T(8,128)(2,1)S(1)} %collective-permute-done.23.other), custom_call_target="tpu_custom_call" | custom-call | flops 10000000000 | bytes 10000000 | tf_op jit(solution)/shard_map/image_units/pallas_call | solution.py:143
  81.0 4.6 %collective-permute-done.25.refs_7_ = bf16[200,1536]{1,0:T(8,128)(2,1)S(1)} collective-permute-done((bf16[200,1536]{1,0:T(8,128)(2,1)}, bf16[200,1536]{1,0:T(8,128)(2,1)S(1)}, u32[]{:S(2)}, u32[]{:S(2)}) %collective-permute-start.25) | collective-permute-done | bytes 614432 | tf_op jit(solution)/shard_map/ppermute | solution.py:22
  85.6 15.2 %score.1 = (f32[512,2048]{1,0:T(8,128)}, f32[1,2048]{1,0:T(1,128)S(1)}, f32[512,1]{1,0:T(8,128)S(1)}) custom-call(s32[1]{0:T(128)} %bitcast.core, f32[1]{0:T(128)S(6)} %copy.13.scale, bf16[1280,640]{1,0:T(8,128)(2,1)S(1)} %get-tuple-element.46.own, bf16[1280,640]{1,0:T(8,128)(2,1)S(1)} %collective-permute-done.20.other, ...), custom_call_target="tpu_custom_call" | custom-call | tf_op jit(solution)/shard_map/score/pallas_call | solution.py:235
  102.5 2.4 %collective-permute-start.27 = (f32[4,128]{1,0:T(4,128)S(1)}, f32[4,128]{1,0:T(4,128)S(1)}, u32[]{:S(2)}, u32[]{:S(2)}) collective-permute-start(f32[4,128]{1,0:T(4,128)S(1)} %log_add_fusion.2), channel_id=1, source_target_pairs={{0,2},{2,4},{4,6},{6,0},{1,3},{3,5},{5,7},{7,1},{8,10},{10,12},{12... | collective-permute-start | bytes 6152 | tf_op jit(solution)/shard_map/ppermute | solution.py:22
  105.9 2.6 %collective-permute-start.29 = (f32[4,128]{1,0:T(4,128)S(1)}, f32[4,128]{1,0:T(4,128)S(1)}, u32[]{:S(2)}, u32[]{:S(2)}) collective-permute-start(f32[4,128]{1,0:T(4,128)S(1)} %log_add_fusion.2), channel_id=1, source_target_pairs={{0,4},{2,6},{4,0},{6,2},{1,5},{3,7},{5,1},{7,3},{8,12},{10,14},{12... | collective-permute-start | bytes 6152 | tf_op jit(solution)/shard_map/ppermute | solution.py:22
  109.1 9.0 %all-to-all-start.1 = ((f32[32,16,128]{2,1,0:T(8,128)}), f32[32,16,128]{2,1,0:T(8,128)S(1)}, u32[]{:S(2)}, u32[]{:S(2)}) async-start(f32[32,16,128]{2,1,0:T(8,128)} %broadcast_in_dim.8), calls=%async_computation.1 | async-start | bytes 524288 | tf_op jit(solution)/shard_map/all_to_all | solution.py:371
  118.3 3.4 %minus.2 = f32[512,2048]{1,0:T(8,128)} custom-call(f32[512,2048]{1,0:T(8,128)} %get-tuple-element.53.logits, f32[512,1]{1,0:T(8,128)S(1)} %copy.8.lse), custom_call_target="tpu_custom_call" | custom-call | tf_op jit(solution)/shard_map/minus/pallas_call | solution.py:281
  121.8 7.9 %all-to-all-done.1 = f32[32,16,128]{2,1,0:T(8,128)S(1)} async-done(((f32[32,16,128]{2,1,0:T(8,128)}), f32[32,16,128]{2,1,0:T(8,128)S(1)}, u32[]{:S(2)}, u32[]{:S(2)}) %all-to-all-start.1) | async-done | bytes 262176 | tf_op jit(solution)/shard_map/all_to_all | solution.py:371
  129.8 3.5 %minus.3 = f32[512,2048]{1,0:T(8,128)} custom-call(f32[512,2048]{1,0:T(8,128)} %get-tuple-element.53.logits, f32[1,2048]{1,0:T(1,128)S(1)} %bitcast.19), custom_call_target="tpu_custom_call" | custom-call | tf_op jit(solution)/shard_map/minus/pallas_call | solution.py:281
  (102 shorter events, 31.0 us)
Async XLA Ops:
  1.6 9.3 %collective-permute-start = (bf16[40,1152]{1,0:T(8,128)(2,1)S(1)}, bf16[40,1152]{1,0:T(8,128)(2,1)S(1)}, u32[]{:S(2)}, u32[]{:S(2)}) collective-permute-start(bf16[40,1152]{1,0:T(8,128)(2,1)S(1)} %pad_maximum_fusion.2.refs_0_), channel_id=1, source_target_pairs={{0,8},{8,16},{16,24},{24,0},{1,9},{9,17},{17,25},{25,1},{2,10},{10... | collective-permute-start | bytes 276488 | tf_op jit(solution)/shard_map/ppermute | solution.py:22
  3.1 7.7 %collective-permute-start.1 = (bf16[40,1152]{1,0:T(8,128)(2,1)S(1)}, bf16[40,1152]{1,0:T(8,128)(2,1)S(1)}, u32[]{:S(2)}, u32[]{:S(2)}) collective-permute-start(bf16[40,1152]{1,0:T(8,128)(2,1)S(1)} %pad_maximum_fusion.2.refs_0_), channel_id=1, source_target_pairs={{0,24},{8,0},{16,8},{24,16},{1,25},{9,1},{17,9},{25,17},{2,26},{10... | collective-permute-start | bytes 276488 | tf_op jit(solution)/shard_map/ppermute | solution.py:22
  15.3 18.2 %collective-permute-start.9 = (bf16[120,1536]{1,0:T(8,128)(2,1)}, bf16[120,1536]{1,0:T(8,128)(2,1)}, u32[]{:S(2)}, u32[]{:S(2)}) collective-permute-start(bf16[120,1536]{1,0:T(8,128)(2,1)} %pad_maximum_fusion.1.refs_0_), channel_id=1, source_target_pairs={{0,8},{8,16},{16,24},{24,0},{1,9},{9,17},{17,25},{25,1},{2,10},{10... | collective-permute-start | bytes 1105928 | tf_op jit(solution)/shard_map/ppermute | solution.py:22
  15.9 17.6 %collective-permute-start.5 = (bf16[160,1152]{1,0:T(8,128)(2,1)S(1)}, bf16[160,1152]{1,0:T(8,128)(2,1)}, u32[]{:S(2)}, u32[]{:S(2)}) collective-permute-start(bf16[160,1152]{1,0:T(8,128)(2,1)S(1)} %join.1.refs_0_), channel_id=1, source_target_pairs={{0,32},{32,64},{64,96},{96,128},{128,160},{160,192},{192,224},{224... | collective-permute-start | bytes 1105928 | tf_op jit(solution)/shard_map/ppermute | solution.py:22
  18.9 14.6 %collective-permute-start.6 = (bf16[160,1152]{1,0:T(8,128)(2,1)S(1)}, bf16[160,1152]{1,0:T(8,128)(2,1)}, u32[]{:S(2)}, u32[]{:S(2)}) collective-permute-start(bf16[160,1152]{1,0:T(8,128)(2,1)S(1)} %join.1.refs_0_), channel_id=1, source_target_pairs={{0,224},{32,0},{64,32},{96,64},{128,96},{160,128},{192,160},{224,1... | collective-permute-start | bytes 1105928 | tf_op jit(solution)/shard_map/ppermute | solution.py:22
  20.7 43.4 %all-to-all-start = ((bf16[4,208,1792]{2,1,0:T(8,128)(2,1)}), bf16[4,208,1792]{2,1,0:T(8,128)(2,1)S(1)}, u32[]{:S(2)}, u32[]{:S(2)}) async-start(bf16[4,208,1792]{2,1,0:T(8,128)(2,1)} %broadcast_in_dim.6), calls=%async_computation | async-start | bytes 5963776 | tf_op jit(solution)/shard_map/all_to_all | solution.py:323
  33.5 8.0 %collective-permute-start.12 = (bf16[40,1536]{1,0:T(8,128)(2,1)S(1)}, bf16[40,1536]{1,0:T(8,128)(2,1)S(1)}, u32[]{:S(2)}, u32[]{:S(2)}) collective-permute-start(bf16[40,1536]{1,0:T(8,128)(2,1)S(1)} %collective-permute-done.7), channel_id=1, source_target_pairs={{0,32},{32,64},{64,96},{96,128},{128,160},{160,192},{192,224},{224... | collective-permute-start | bytes 368648 | tf_op jit(solution)/shard_map/ppermute | solution.py:22
  35.6 13.5 %collective-permute-start.15 = (bf16[120,1536]{1,0:T(8,128)(2,1)}, bf16[120,1536]{1,0:T(8,128)(2,1)S(1)}, u32[]{:S(2)}, u32[]{:S(2)}) collective-permute-start(bf16[120,1536]{1,0:T(8,128)(2,1)} %pad_maximum_fusion.1.refs_0_), channel_id=1, source_target_pairs={{0,24},{8,0},{16,8},{24,16},{1,25},{9,1},{17,9},{25,17},{2,26},{10... | collective-permute-start | bytes 1105928 | tf_op jit(solution)/shard_map/ppermute | solution.py:22
  38.2 10.8 %collective-permute-start.10 = (bf16[160,1152]{1,0:T(8,128)(2,1)}, bf16[160,1152]{1,0:T(8,128)(2,1)S(1)}, u32[]{:S(2)}, u32[]{:S(2)}) collective-permute-start(bf16[160,1152]{1,0:T(8,128)(2,1)} %collective-permute-done.5.refs_1_), channel_id=1, source_target_pairs={{0,32},{32,64},{64,96},{96,128},{128,160},{160,192},{192,224},{224... | collective-permute-start | bytes 1105928 | tf_op jit(solution)/shard_map/ppermute | solution.py:22
  41.5 7.7 %collective-permute-start.11 = (bf16[160,1152]{1,0:T(8,128)(2,1)}, bf16[160,1152]{1,0:T(8,128)(2,1)S(1)}, u32[]{:S(2)}, u32[]{:S(2)}) collective-permute-start(bf16[160,1152]{1,0:T(8,128)(2,1)} %collective-permute-done.6.refs_2_), channel_id=1, source_target_pairs={{0,224},{32,0},{64,32},{96,64},{128,96},{160,128},{192,160},{224,1... | collective-permute-start | bytes 1105928 | tf_op jit(solution)/shard_map/ppermute | solution.py:22
  49.2 13.3 %collective-permute-start.18 = (bf16[200,1536]{1,0:T(8,128)(2,1)S(1)}, bf16[200,1536]{1,0:T(8,128)(2,1)S(1)}, u32[]{:S(2)}, u32[]{:S(2)}) collective-permute-start(bf16[200,1536]{1,0:T(8,128)(2,1)S(1)} %constant_dynamic-update-slice_fusion.refs_4_), channel_id=1, source_target_pairs={{0,8},{8,16},{16,24},{24,0},{1,9},{9,17},{17,25},{25,1},{2,10},{10... | collective-permute-start | bytes 1843208 | tf_op jit(solution)/shard_map/ppermute | solution.py:22
  49.2 14.9 %collective-permute-start.19 = (bf16[200,1536]{1,0:T(8,128)(2,1)S(1)}, bf16[200,1536]{1,0:T(8,128)(2,1)}, u32[]{:S(2)}, u32[]{:S(2)}) collective-permute-start(bf16[200,1536]{1,0:T(8,128)(2,1)S(1)} %constant_dynamic-update-slice_fusion.refs_4_), channel_id=1, source_target_pairs={{0,24},{8,0},{16,8},{24,16},{1,25},{9,1},{17,9},{25,17},{2,26},{10... | collective-permute-start | bytes 1843208 | tf_op jit(solution)/shard_map/ppermute | solution.py:22
  52.4 7.8 %collective-permute-start.16 = (bf16[160,1152]{1,0:T(8,128)(2,1)S(1)}, bf16[160,1152]{1,0:T(8,128)(2,1)S(1)}, u32[]{:S(2)}, u32[]{:S(2)}) collective-permute-start(bf16[160,1152]{1,0:T(8,128)(2,1)S(1)} %collective-permute-done.10.refs_3_), channel_id=1, source_target_pairs={{0,32},{32,64},{64,96},{96,128},{128,160},{160,192},{192,224},{224... | collective-permute-start | bytes 1105928 | tf_op jit(solution)/shard_map/ppermute | solution.py:22
  54.4 8.0 %collective-permute-start.17 = (bf16[160,1152]{1,0:T(8,128)(2,1)S(1)}, bf16[160,1152]{1,0:T(8,128)(2,1)S(1)}, u32[]{:S(2)}, u32[]{:S(2)}) collective-permute-start(bf16[160,1152]{1,0:T(8,128)(2,1)S(1)} %collective-permute-done.11.refs_4_), channel_id=1, source_target_pairs={{0,224},{32,0},{64,32},{96,64},{128,96},{160,128},{192,160},{224,1... | collective-permute-start | bytes 1105928 | tf_op jit(solution)/shard_map/ppermute | solution.py:22
  64.1 13.0 %collective-permute-start.23 = (bf16[832,1792]{1,0:T(8,128)(2,1)S(1)}, bf16[832,1792]{1,0:T(8,128)(2,1)S(1)}, u32[]{:S(2)}, u32[]{:S(2)}) collective-permute-start(bf16[832,1792]{1,0:T(8,128)(2,1)S(1)} %bitcast.17), channel_id=1, source_target_pairs={{0,1},{1,0},{2,3},{3,2},{4,5},{5,4},{6,7},{7,6},{8,9},{9,8},{10,11... | collective-permute-start | bytes 8945672 | tf_op jit(solution)/shard_map/ppermute | solution.py:22
  66.0 19.7 %collective-permute-start.20 = (bf16[1280,640]{1,0:T(8,128)(2,1)S(1)}, bf16[1280,640]{1,0:T(8,128)(2,1)S(1)}, u32[]{:S(2)}, u32[]{:S(2)}) collective-permute-start(bf16[1280,640]{1,0:T(8,128)(2,1)S(1)} %get-tuple-element.46.own), channel_id=1, source_target_pairs={{0,1},{1,0},{2,3},{3,2},{4,5},{5,4},{6,7},{7,6},{8,9},{9,8},{10,11... | collective-permute-start | bytes 4915208 | tf_op jit(solution)/shard_map/ppermute | solution.py:22
  66.5 10.6 %collective-permute-start.21 = (bf16[160,1152]{1,0:T(8,128)(2,1)S(1)}, bf16[160,1152]{1,0:T(8,128)(2,1)S(1)}, u32[]{:S(2)}, u32[]{:S(2)}) collective-permute-start(bf16[160,1152]{1,0:T(8,128)(2,1)S(1)} %copy-done.14), channel_id=1, source_target_pairs={{0,32},{32,64},{64,96},{96,128},{128,160},{160,192},{192,224},{224... | collective-permute-start | bytes 1105928 | tf_op jit(solution)/shard_map/ppermute | solution.py:22
  69.2 11.8 %collective-permute-start.24 = (bf16[120,1536]{1,0:T(8,128)(2,1)}, bf16[120,1536]{1,0:T(8,128)(2,1)S(1)}, u32[]{:S(2)}, u32[]{:S(2)}) collective-permute-start(bf16[120,1536]{1,0:T(8,128)(2,1)} %collective-permute-done.9.refs_1_), channel_id=1, source_target_pairs={{0,8},{8,16},{16,24},{24,0},{1,9},{9,17},{17,25},{25,1},{2,10},{10... | collective-permute-start | bytes 1105928 | tf_op jit(solution)/shard_map/ppermute | solution.py:22
  69.3 16.4 %collective-permute-start.25 = (bf16[200,1536]{1,0:T(8,128)(2,1)}, bf16[200,1536]{1,0:T(8,128)(2,1)S(1)}, u32[]{:S(2)}, u32[]{:S(2)}) collective-permute-start(bf16[200,1536]{1,0:T(8,128)(2,1)} %collective-permute-done.19.refs_6_), channel_id=1, source_target_pairs={{0,24},{8,0},{16,8},{24,16},{1,25},{9,1},{17,9},{25,17},{2,26},{10... | collective-permute-start | bytes 1843208 | tf_op jit(solution)/shard_map/ppermute | solution.py:22
  77.1 8.5 %collective-permute-start.22 = (bf16[160,1152]{1,0:T(8,128)(2,1)S(1)}, bf16[160,1152]{1,0:T(8,128)(2,1)S(1)}, u32[]{:S(2)}, u32[]{:S(2)}) collective-permute-start(bf16[160,1152]{1,0:T(8,128)(2,1)S(1)} %collective-permute-done.21.far_own), channel_id=1, source_target_pairs={{0,1},{1,0},{2,3},{3,2},{4,5},{5,4},{6,7},{7,6},{8,9},{9,8},{10,11... | collective-permute-start | bytes 1105928 | tf_op jit(solution)/shard_map/ppermute | solution.py:22
  102.5 15.6 %collective-permute-start.27 = (f32[4,128]{1,0:T(4,128)S(1)}, f32[4,128]{1,0:T(4,128)S(1)}, u32[]{:S(2)}, u32[]{:S(2)}) collective-permute-start(f32[4,128]{1,0:T(4,128)S(1)} %log_add_fusion.2), channel_id=1, source_target_pairs={{0,2},{2,4},{4,6},{6,0},{1,3},{3,5},{5,7},{7,1},{8,10},{10,12},{12... | collective-permute-start | bytes 6152 | tf_op jit(solution)/shard_map/ppermute | solution.py:22
  104.9 13.2 %collective-permute-start.28 = (f32[4,128]{1,0:T(4,128)S(1)}, f32[4,128]{1,0:T(4,128)S(1)}, u32[]{:S(2)}, u32[]{:S(2)}) collective-permute-start(f32[4,128]{1,0:T(4,128)S(1)} %log_add_fusion.2), channel_id=1, source_target_pairs={{0,6},{2,0},{4,2},{6,4},{1,7},{3,1},{5,3},{7,5},{8,14},{10,8},{12,... | collective-permute-start | bytes 6152 | tf_op jit(solution)/shard_map/ppermute | solution.py:22
  105.9 12.3 %collective-permute-start.29 = (f32[4,128]{1,0:T(4,128)S(1)}, f32[4,128]{1,0:T(4,128)S(1)}, u32[]{:S(2)}, u32[]{:S(2)}) collective-permute-start(f32[4,128]{1,0:T(4,128)S(1)} %log_add_fusion.2), channel_id=1, source_target_pairs={{0,4},{2,6},{4,0},{6,2},{1,5},{3,7},{5,1},{7,3},{8,12},{10,14},{12... | collective-permute-start | bytes 6152 | tf_op jit(solution)/shard_map/ppermute | solution.py:22
  109.1 20.6 %all-to-all-start.1 = ((f32[32,16,128]{2,1,0:T(8,128)}), f32[32,16,128]{2,1,0:T(8,128)S(1)}, u32[]{:S(2)}, u32[]{:S(2)}) async-start(f32[32,16,128]{2,1,0:T(8,128)} %broadcast_in_dim.8), calls=%async_computation.1 | async-start | bytes 524288 | tf_op jit(solution)/shard_map/all_to_all | solution.py:371
  (24 other events, 133.2 us)

commit v2 on v1

--- a/solution.py
+++ b/solution.py
@@ -14,7 +14,6 @@
 ROWS_A = 512
 TILE = 512
 VMEM_LIMIT = 24 * 1024 * 1024
-BUSY = pl.CostEstimate(flops=10**10, bytes_accessed=10**7, transcendentals=0)
 
 
 def shift(value, axis, step):
@@ -120,7 +119,6 @@
         ],
         compiler_params=params(),
         name="split_chunks",
-        cost_estimate=BUSY,
     )(*from_hbm(chunks))
 
 
@@ -148,7 +146,6 @@
         out_specs=fixed(rows, own.shape[1] - rows),
         compiler_params=params(),
         name="image_units",
-        cost_estimate=BUSY,
     )(own, other)
 
 

time: 134 us -> 131 us (0.978)
  starting transfers between devices: 55.3 us -> 52.5 us
    all_to_all x1, starting transfers between devices: 8.95 us -> 7.42 us  [on_device(): col_lse = add_exp(lax.all_to_all(spread, IMG, 0, 0)).reshape(-1)]
  transfers between devices with their start and end apart: 32 -> 32, of which waited for: 13 -> 12; matrix products, arithmetic and copies ran while one was open for 4% -> 4% of each run, Pallas kernels for 7% -> 7%
where the time goes in v2:
time: 131 us
  starting transfers between devices  52.5 us (40%)
  waiting for transfers between devices  38.7 us (30%)
  Pallas kernels  28 us (21%)
  local copies, waits for them, and re-layouts  7.35 us (6%)
  other arithmetic  2.25 us (2%)
  between operations  1.86 us (1%)
    ppermute x30, starting transfers between devices, shift(): lax.ppermute(value, axis, [(i, (i + step) % count) for i in range(count)])  40.6 us
    ppermute x30, waiting for transfers between devices, shift(): lax.ppermute(value, axis, [(i, (i + step) % count) for i in range(count)])  30.8 us
    pallas_call x1, Pallas kernels, score(): pl.pallas_call(functools.partial(score_kernel, depth), out_shape=(pltpu.H...  15.2 us
    all_to_all x1, waiting for transfers between devices, on_device(): col_lse = add_exp(lax.all_to_all(spread, IMG, 0, 0)).reshape(-1)  7.93 us
    all_to_all x1, starting transfers between devices, on_device(): col_lse = add_exp(lax.all_to_all(spread, IMG, 0, 0)).reshape(-1)  7.42 us
    pallas_call x2, Pallas kernels, minus(): pl.pallas_call(minus_kernel, out_shape=pltpu.HBM((rows, columns), jnp.flo...  6.95 us
    all_to_all x1, starting transfers between devices, on_device(): lax.all_to_all(spread, 'y', 0, 0).reshape(-1, image_lines.shape[1])  4.46 us
    pallas_call x1, Pallas kernels, image_units(): pl.pallas_call(functools.partial(image_kernel, rows), out_shape=jax.Shape...  3.09 us
  transfers between devices with their start and end apart: 32, of which 12 were waited for; matrix products, arithmetic and copies ran while one was open for 4% of the time, Pallas kernels for 7%

profile of v2, /device:TPU:32, one launch (start us, length us, event | category | flops | bytes accessed | tf_op | source)
XLA Modules:
  0.0 130.7 jit_solution(7752008560815668434)
XLA Ops:
  15.9 3.0 %collective-permute-start.5 = (bf16[160,1152]{1,0:T(8,128)(2,1)S(1)}, bf16[160,1152]{1,0:T(8,128)(2,1)}, u32[]{:S(2)}, u32[]{:S(2)}) collective-permute-start(bf16[160,1152]{1,0:T(8,128)(2,1)S(1)} %join.1.refs_0_), channel_id=1, source_target_pairs={{0,32},{32,64},{64,96},{96,128},{128,160},{160,192},{192,224},{224... | collective-permute-start | bytes 1105928 | tf_op jit(solution)/shard_map/ppermute | solution.py:21
  20.7 4.5 %all-to-all-start = ((bf16[4,208,1792]{2,1,0:T(8,128)(2,1)}), bf16[4,208,1792]{2,1,0:T(8,128)(2,1)S(1)}, u32[]{:S(2)}, u32[]{:S(2)}) async-start(bf16[4,208,1792]{2,1,0:T(8,128)(2,1)} %broadcast_in_dim.6), calls=%async_computation | async-start | bytes 5963776 | tf_op jit(solution)/shard_map/all_to_all | solution.py:320
  25.2 3.2 %collective-permute-start.7 = (bf16[40,1536]{1,0:T(8,128)(2,1)}, bf16[40,1536]{1,0:T(8,128)(2,1)S(1)}, u32[]{:S(2)}, u32[]{:S(2)}) collective-permute-start(bf16[40,1536]{1,0:T(8,128)(2,1)} %copy-done.11), channel_id=1, source_target_pairs={{0,32},{32,64},{64,96},{96,128},{128,160},{160,192},{192,224},{224... | collective-permute-start | bytes 368648 | tf_op jit(solution)/shard_map/ppermute | solution.py:21
  28.4 2.9 %collective-permute-done.7 = bf16[40,1536]{1,0:T(8,128)(2,1)S(1)} collective-permute-done((bf16[40,1536]{1,0:T(8,128)(2,1)}, bf16[40,1536]{1,0:T(8,128)(2,1)S(1)}, u32[]{:S(2)}, u32[]{:S(2)}) %collective-permute-start.7) | collective-permute-done | bytes 122912 | tf_op jit(solution)/shard_map/ppermute | solution.py:21
  31.3 2.2 %collective-permute-done.8 = bf16[40,1536]{1,0:T(8,128)(2,1)S(1)} collective-permute-done((bf16[40,1536]{1,0:T(8,128)(2,1)}, bf16[40,1536]{1,0:T(8,128)(2,1)S(1)}, u32[]{:S(2)}, u32[]{:S(2)}) %collective-permute-start.8) | collective-permute-done | bytes 122912 | tf_op jit(solution)/shard_map/ppermute | solution.py:21
  33.5 2.1 %collective-permute-start.12 = (bf16[40,1536]{1,0:T(8,128)(2,1)S(1)}, bf16[40,1536]{1,0:T(8,128)(2,1)S(1)}, u32[]{:S(2)}, u32[]{:S(2)}) collective-permute-start(bf16[40,1536]{1,0:T(8,128)(2,1)S(1)} %collective-permute-done.7), channel_id=1, source_target_pairs={{0,32},{32,64},{64,96},{96,128},{128,160},{160,192},{192,224},{224... | collective-permute-start | bytes 368648 | tf_op jit(solution)/shard_map/ppermute | solution.py:21
  35.6 2.6 %collective-permute-start.15 = (bf16[120,1536]{1,0:T(8,128)(2,1)}, bf16[120,1536]{1,0:T(8,128)(2,1)S(1)}, u32[]{:S(2)}, u32[]{:S(2)}) collective-permute-start(bf16[120,1536]{1,0:T(8,128)(2,1)} %pad_maximum_fusion.1.refs_0_), channel_id=1, source_target_pairs={{0,24},{8,0},{16,8},{24,16},{1,25},{9,1},{17,9},{25,17},{2,26},{10... | collective-permute-start | bytes 1105928 | tf_op jit(solution)/shard_map/ppermute | solution.py:21
  38.2 3.2 %collective-permute-start.10 = (bf16[160,1152]{1,0:T(8,128)(2,1)}, bf16[160,1152]{1,0:T(8,128)(2,1)S(1)}, u32[]{:S(2)}, u32[]{:S(2)}) collective-permute-start(bf16[160,1152]{1,0:T(8,128)(2,1)} %collective-permute-done.5.refs_1_), channel_id=1, source_target_pairs={{0,32},{32,64},{64,96},{96,128},{128,160},{160,192},{192,224},{224... | collective-permute-start | bytes 1105928 | tf_op jit(solution)/shard_map/ppermute | solution.py:21
  41.5 2.0 %collective-permute-start.13 = (bf16[40,1536]{1,0:T(8,128)(2,1)S(1)}, bf16[40,1536]{1,0:T(8,128)(2,1)S(1)}, u32[]{:S(2)}, u32[]{:S(2)}) collective-permute-start(bf16[40,1536]{1,0:T(8,128)(2,1)S(1)} %collective-permute-done.12), channel_id=1, source_target_pairs={{0,32},{32,64},{64,96},{96,128},{128,160},{160,192},{192,224},{224... | collective-permute-start | bytes 368648 | tf_op jit(solution)/shard_map/ppermute | solution.py:21
  44.6 4.4 %collective-permute-done.13 = bf16[40,1536]{1,0:T(8,128)(2,1)S(1)} collective-permute-done((bf16[40,1536]{1,0:T(8,128)(2,1)S(1)}, bf16[40,1536]{1,0:T(8,128)(2,1)S(1)}, u32[]{:S(2)}, u32[]{:S(2)}) %collective-permute-start.13) | collective-permute-done | bytes 122912 | tf_op jit(solution)/shard_map/ppermute | solution.py:21
  49.2 3.2 %collective-permute-start.19 = (bf16[200,1536]{1,0:T(8,128)(2,1)S(1)}, bf16[200,1536]{1,0:T(8,128)(2,1)}, u32[]{:S(2)}, u32[]{:S(2)}) collective-permute-start(bf16[200,1536]{1,0:T(8,128)(2,1)S(1)} %constant_dynamic-update-slice_fusion.refs_4_), channel_id=1, source_target_pairs={{0,24},{8,0},{16,8},{24,16},{1,25},{9,1},{17,9},{25,17},{2,26},{10... | collective-permute-start | bytes 1843208 | tf_op jit(solution)/shard_map/ppermute | solution.py:21
  54.7 5.5 %collective-permute-done.16.refs_5_ = bf16[160,1152]{1,0:T(8,128)(2,1)S(1)} collective-permute-done((bf16[160,1152]{1,0:T(8,128)(2,1)S(1)}, bf16[160,1152]{1,0:T(8,128)(2,1)S(1)}, u32[]{:S(2)}, u32[]{:S(2)}) %collective-permute-start.16) | collective-permute-done | bytes 368672 | tf_op jit(solution)/shard_map/ppermute | solution.py:21
  60.2 2.2 %collective-permute-done.17.refs_6_ = bf16[160,1152]{1,0:T(8,128)(2,1)S(1)} collective-permute-done((bf16[160,1152]{1,0:T(8,128)(2,1)S(1)}, bf16[160,1152]{1,0:T(8,128)(2,1)S(1)}, u32[]{:S(2)}, u32[]{:S(2)}) %collective-permute-start.17) | collective-permute-done | bytes 368672 | tf_op jit(solution)/shard_map/ppermute | solution.py:21
  66.5 2.0 %collective-permute-start.21 = (bf16[160,1152]{1,0:T(8,128)(2,1)S(1)}, bf16[160,1152]{1,0:T(8,128)(2,1)S(1)}, u32[]{:S(2)}, u32[]{:S(2)}) collective-permute-start(bf16[160,1152]{1,0:T(8,128)(2,1)S(1)} %copy-done.7), channel_id=1, source_target_pairs={{0,32},{32,64},{64,96},{96,128},{128,160},{160,192},{192,224},{224... | collective-permute-start | bytes 1105928 | tf_op jit(solution)/shard_map/ppermute | solution.py:21
  70.6 6.5 %collective-permute-done.21.far_own = bf16[160,1152]{1,0:T(8,128)(2,1)S(1)} collective-permute-done((bf16[160,1152]{1,0:T(8,128)(2,1)S(1)}, bf16[160,1152]{1,0:T(8,128)(2,1)S(1)}, u32[]{:S(2)}, u32[]{:S(2)}) %collective-permute-start.21) | collective-permute-done | bytes 368672 | tf_op jit(solution)/shard_map/ppermute | solution.py:21
  77.8 3.1 %image_units.1.image = bf16[512,1280]{1,0:T(8,128)(2,1)S(1)} custom-call(bf16[832,1792]{1,0:T(8,128)(2,1)S(1)} %bitcast.18, bf16[832,1792]{1,0:T(8,128)(2,1)S(1)} %collective-permute-done.23.other), custom_call_target="tpu_custom_call" | custom-call | tf_op jit(solution)/shard_map/image_units/pallas_call | solution.py:141
  80.9 3.4 %collective-permute-done.25.refs_7_ = bf16[200,1536]{1,0:T(8,128)(2,1)S(1)} collective-permute-done((bf16[200,1536]{1,0:T(8,128)(2,1)}, bf16[200,1536]{1,0:T(8,128)(2,1)S(1)}, u32[]{:S(2)}, u32[]{:S(2)}) %collective-permute-start.25) | collective-permute-done | bytes 614432 | tf_op jit(solution)/shard_map/ppermute | solution.py:21
  84.3 15.2 %score.1 = (f32[512,2048]{1,0:T(8,128)}, f32[1,2048]{1,0:T(1,128)S(1)}, f32[512,1]{1,0:T(8,128)S(1)}) custom-call(s32[1]{0:T(128)} %bitcast.core, f32[1]{0:T(128)S(6)} %copy.13.scale, bf16[1280,640]{1,0:T(8,128)(2,1)S(1)} %get-tuple-element.46.own, bf16[1280,640]{1,0:T(8,128)(2,1)S(1)} %collective-permute-done.20.other, ...), custom_call_target="tpu_custom_call" | custom-call | tf_op jit(solution)/shard_map/score/pallas_call | solution.py:232
  101.2 2.4 %collective-permute-start.27 = (f32[4,128]{1,0:T(4,128)S(1)}, f32[4,128]{1,0:T(4,128)S(1)}, u32[]{:S(2)}, u32[]{:S(2)}) collective-permute-start(f32[4,128]{1,0:T(4,128)S(1)} %log_add_fusion.2), channel_id=1, source_target_pairs={{0,2},{2,4},{4,6},{6,0},{1,3},{3,5},{5,7},{7,1},{8,10},{10,12},{12... | collective-permute-start | bytes 6152 | tf_op jit(solution)/shard_map/ppermute | solution.py:21
  104.6 2.6 %collective-permute-start.29 = (f32[4,128]{1,0:T(4,128)S(1)}, f32[4,128]{1,0:T(4,128)S(1)}, u32[]{:S(2)}, u32[]{:S(2)}) collective-permute-start(f32[4,128]{1,0:T(4,128)S(1)} %log_add_fusion.2), channel_id=1, source_target_pairs={{0,4},{2,6},{4,0},{6,2},{1,5},{3,7},{5,1},{7,3},{8,12},{10,14},{12... | collective-permute-start | bytes 6152 | tf_op jit(solution)/shard_map/ppermute | solution.py:21
  107.8 7.4 %all-to-all-start.1 = ((f32[32,16,128]{2,1,0:T(8,128)}), f32[32,16,128]{2,1,0:T(8,128)S(1)}, u32[]{:S(2)}, u32[]{:S(2)}) async-start(f32[32,16,128]{2,1,0:T(8,128)} %broadcast_in_dim.8), calls=%async_computation.1 | async-start | bytes 524288 | tf_op jit(solution)/shard_map/all_to_all | solution.py:368
  115.5 3.4 %minus.2 = f32[512,2048]{1,0:T(8,128)} custom-call(f32[512,2048]{1,0:T(8,128)} %get-tuple-element.53.logits, f32[512,1]{1,0:T(8,128)S(1)} %copy.8.lse), custom_call_target="tpu_custom_call" | custom-call | tf_op jit(solution)/shard_map/minus/pallas_call | solution.py:278
  118.9 7.9 %all-to-all-done.1 = f32[32,16,128]{2,1,0:T(8,128)S(1)} async-done(((f32[32,16,128]{2,1,0:T(8,128)}), f32[32,16,128]{2,1,0:T(8,128)S(1)}, u32[]{:S(2)}, u32[]{:S(2)}) %all-to-all-start.1) | async-done | bytes 262176 | tf_op jit(solution)/shard_map/all_to_all | solution.py:368
  127.0 3.5 %minus.3 = f32[512,2048]{1,0:T(8,128)} custom-call(f32[512,2048]{1,0:T(8,128)} %get-tuple-element.53.logits, f32[1,2048]{1,0:T(1,128)S(1)} %bitcast.19), custom_call_target="tpu_custom_call" | custom-call | tf_op jit(solution)/shard_map/minus/pallas_call | solution.py:278
  (102 shorter events, 30.2 us)
Async XLA Ops:
  1.6 9.3 %collective-permute-start = (bf16[40,1152]{1,0:T(8,128)(2,1)S(1)}, bf16[40,1152]{1,0:T(8,128)(2,1)S(1)}, u32[]{:S(2)}, u32[]{:S(2)}) collective-permute-start(bf16[40,1152]{1,0:T(8,128)(2,1)S(1)} %pad_maximum_fusion.2.refs_0_), channel_id=1, source_target_pairs={{0,8},{8,16},{16,24},{24,0},{1,9},{9,17},{17,25},{25,1},{2,10},{10... | collective-permute-start | bytes 276488 | tf_op jit(solution)/shard_map/ppermute | solution.py:21
  3.1 7.7 %collective-permute-start.1 = (bf16[40,1152]{1,0:T(8,128)(2,1)S(1)}, bf16[40,1152]{1,0:T(8,128)(2,1)S(1)}, u32[]{:S(2)}, u32[]{:S(2)}) collective-permute-start(bf16[40,1152]{1,0:T(8,128)(2,1)S(1)} %pad_maximum_fusion.2.refs_0_), channel_id=1, source_target_pairs={{0,24},{8,0},{16,8},{24,16},{1,25},{9,1},{17,9},{25,17},{2,26},{10... | collective-permute-start | bytes 276488 | tf_op jit(solution)/shard_map/ppermute | solution.py:21
  15.3 18.2 %collective-permute-start.9 = (bf16[120,1536]{1,0:T(8,128)(2,1)}, bf16[120,1536]{1,0:T(8,128)(2,1)}, u32[]{:S(2)}, u32[]{:S(2)}) collective-permute-start(bf16[120,1536]{1,0:T(8,128)(2,1)} %pad_maximum_fusion.1.refs_0_), channel_id=1, source_target_pairs={{0,8},{8,16},{16,24},{24,0},{1,9},{9,17},{17,25},{25,1},{2,10},{10... | collective-permute-start | bytes 1105928 | tf_op jit(solution)/shard_map/ppermute | solution.py:21
  15.9 17.6 %collective-permute-start.5 = (bf16[160,1152]{1,0:T(8,128)(2,1)S(1)}, bf16[160,1152]{1,0:T(8,128)(2,1)}, u32[]{:S(2)}, u32[]{:S(2)}) collective-permute-start(bf16[160,1152]{1,0:T(8,128)(2,1)S(1)} %join.1.refs_0_), channel_id=1, source_target_pairs={{0,32},{32,64},{64,96},{96,128},{128,160},{160,192},{192,224},{224... | collective-permute-start | bytes 1105928 | tf_op jit(solution)/shard_map/ppermute | solution.py:21
  18.9 14.6 %collective-permute-start.6 = (bf16[160,1152]{1,0:T(8,128)(2,1)S(1)}, bf16[160,1152]{1,0:T(8,128)(2,1)}, u32[]{:S(2)}, u32[]{:S(2)}) collective-permute-start(bf16[160,1152]{1,0:T(8,128)(2,1)S(1)} %join.1.refs_0_), channel_id=1, source_target_pairs={{0,224},{32,0},{64,32},{96,64},{128,96},{160,128},{192,160},{224,1... | collective-permute-start | bytes 1105928 | tf_op jit(solution)/shard_map/ppermute | solution.py:21
  20.7 43.4 %all-to-all-start = ((bf16[4,208,1792]{2,1,0:T(8,128)(2,1)}), bf16[4,208,1792]{2,1,0:T(8,128)(2,1)S(1)}, u32[]{:S(2)}, u32[]{:S(2)}) async-start(bf16[4,208,1792]{2,1,0:T(8,128)(2,1)} %broadcast_in_dim.6), calls=%async_computation | async-start | bytes 5963776 | tf_op jit(solution)/shard_map/all_to_all | solution.py:320
  33.5 8.0 %collective-permute-start.12 = (bf16[40,1536]{1,0:T(8,128)(2,1)S(1)}, bf16[40,1536]{1,0:T(8,128)(2,1)S(1)}, u32[]{:S(2)}, u32[]{:S(2)}) collective-permute-start(bf16[40,1536]{1,0:T(8,128)(2,1)S(1)} %collective-permute-done.7), channel_id=1, source_target_pairs={{0,32},{32,64},{64,96},{96,128},{128,160},{160,192},{192,224},{224... | collective-permute-start | bytes 368648 | tf_op jit(solution)/shard_map/ppermute | solution.py:21
  35.6 13.5 %collective-permute-start.15 = (bf16[120,1536]{1,0:T(8,128)(2,1)}, bf16[120,1536]{1,0:T(8,128)(2,1)S(1)}, u32[]{:S(2)}, u32[]{:S(2)}) collective-permute-start(bf16[120,1536]{1,0:T(8,128)(2,1)} %pad_maximum_fusion.1.refs_0_), channel_id=1, source_target_pairs={{0,24},{8,0},{16,8},{24,16},{1,25},{9,1},{17,9},{25,17},{2,26},{10... | collective-permute-start | bytes 1105928 | tf_op jit(solution)/shard_map/ppermute | solution.py:21
  38.2 10.8 %collective-permute-start.10 = (bf16[160,1152]{1,0:T(8,128)(2,1)}, bf16[160,1152]{1,0:T(8,128)(2,1)S(1)}, u32[]{:S(2)}, u32[]{:S(2)}) collective-permute-start(bf16[160,1152]{1,0:T(8,128)(2,1)} %collective-permute-done.5.refs_1_), channel_id=1, source_target_pairs={{0,32},{32,64},{64,96},{96,128},{128,160},{160,192},{192,224},{224... | collective-permute-start | bytes 1105928 | tf_op jit(solution)/shard_map/ppermute | solution.py:21
  41.5 7.7 %collective-permute-start.11 = (bf16[160,1152]{1,0:T(8,128)(2,1)}, bf16[160,1152]{1,0:T(8,128)(2,1)S(1)}, u32[]{:S(2)}, u32[]{:S(2)}) collective-permute-start(bf16[160,1152]{1,0:T(8,128)(2,1)} %collective-permute-done.6.refs_2_), channel_id=1, source_target_pairs={{0,224},{32,0},{64,32},{96,64},{128,96},{160,128},{192,160},{224,1... | collective-permute-start | bytes 1105928 | tf_op jit(solution)/shard_map/ppermute | solution.py:21
  41.5 7.5 %collective-permute-start.13 = (bf16[40,1536]{1,0:T(8,128)(2,1)S(1)}, bf16[40,1536]{1,0:T(8,128)(2,1)S(1)}, u32[]{:S(2)}, u32[]{:S(2)}) collective-permute-start(bf16[40,1536]{1,0:T(8,128)(2,1)S(1)} %collective-permute-done.12), channel_id=1, source_target_pairs={{0,32},{32,64},{64,96},{96,128},{128,160},{160,192},{192,224},{224... | collective-permute-start | bytes 368648 | tf_op jit(solution)/shard_map/ppermute | solution.py:21
  49.2 13.3 %collective-permute-start.18 = (bf16[200,1536]{1,0:T(8,128)(2,1)S(1)}, bf16[200,1536]{1,0:T(8,128)(2,1)S(1)}, u32[]{:S(2)}, u32[]{:S(2)}) collective-permute-start(bf16[200,1536]{1,0:T(8,128)(2,1)S(1)} %constant_dynamic-update-slice_fusion.refs_4_), channel_id=1, source_target_pairs={{0,8},{8,16},{16,24},{24,0},{1,9},{9,17},{17,25},{25,1},{2,10},{10... | collective-permute-start | bytes 1843208 | tf_op jit(solution)/shard_map/ppermute | solution.py:21
  49.2 14.9 %collective-permute-start.19 = (bf16[200,1536]{1,0:T(8,128)(2,1)S(1)}, bf16[200,1536]{1,0:T(8,128)(2,1)}, u32[]{:S(2)}, u32[]{:S(2)}) collective-permute-start(bf16[200,1536]{1,0:T(8,128)(2,1)S(1)} %constant_dynamic-update-slice_fusion.refs_4_), channel_id=1, source_target_pairs={{0,24},{8,0},{16,8},{24,16},{1,25},{9,1},{17,9},{25,17},{2,26},{10... | collective-permute-start | bytes 1843208 | tf_op jit(solution)/shard_map/ppermute | solution.py:21
  52.4 7.8 %collective-permute-start.16 = (bf16[160,1152]{1,0:T(8,128)(2,1)S(1)}, bf16[160,1152]{1,0:T(8,128)(2,1)S(1)}, u32[]{:S(2)}, u32[]{:S(2)}) collective-permute-start(bf16[160,1152]{1,0:T(8,128)(2,1)S(1)} %collective-permute-done.10.refs_3_), channel_id=1, source_target_pairs={{0,32},{32,64},{64,96},{96,128},{128,160},{160,192},{192,224},{224... | collective-permute-start | bytes 1105928 | tf_op jit(solution)/shard_map/ppermute | solution.py:21
  54.4 8.0 %collective-permute-start.17 = (bf16[160,1152]{1,0:T(8,128)(2,1)S(1)}, bf16[160,1152]{1,0:T(8,128)(2,1)S(1)}, u32[]{:S(2)}, u32[]{:S(2)}) collective-permute-start(bf16[160,1152]{1,0:T(8,128)(2,1)S(1)} %collective-permute-done.11.refs_4_), channel_id=1, source_target_pairs={{0,224},{32,0},{64,32},{96,64},{128,96},{160,128},{192,160},{224,1... | collective-permute-start | bytes 1105928 | tf_op jit(solution)/shard_map/ppermute | solution.py:21
  64.1 13.7 %collective-permute-start.23 = (bf16[832,1792]{1,0:T(8,128)(2,1)S(1)}, bf16[832,1792]{1,0:T(8,128)(2,1)S(1)}, u32[]{:S(2)}, u32[]{:S(2)}) collective-permute-start(bf16[832,1792]{1,0:T(8,128)(2,1)S(1)} %bitcast.17), channel_id=1, source_target_pairs={{0,1},{1,0},{2,3},{3,2},{4,5},{5,4},{6,7},{7,6},{8,9},{9,8},{10,11... | collective-permute-start | bytes 8945672 | tf_op jit(solution)/shard_map/ppermute | solution.py:21
  65.9 18.4 %collective-permute-start.20 = (bf16[1280,640]{1,0:T(8,128)(2,1)S(1)}, bf16[1280,640]{1,0:T(8,128)(2,1)S(1)}, u32[]{:S(2)}, u32[]{:S(2)}) collective-permute-start(bf16[1280,640]{1,0:T(8,128)(2,1)S(1)} %get-tuple-element.46.own), channel_id=1, source_target_pairs={{0,1},{1,0},{2,3},{3,2},{4,5},{5,4},{6,7},{7,6},{8,9},{9,8},{10,11... | collective-permute-start | bytes 4915208 | tf_op jit(solution)/shard_map/ppermute | solution.py:21
  66.5 10.6 %collective-permute-start.21 = (bf16[160,1152]{1,0:T(8,128)(2,1)S(1)}, bf16[160,1152]{1,0:T(8,128)(2,1)S(1)}, u32[]{:S(2)}, u32[]{:S(2)}) collective-permute-start(bf16[160,1152]{1,0:T(8,128)(2,1)S(1)} %copy-done.7), channel_id=1, source_target_pairs={{0,32},{32,64},{64,96},{96,128},{128,160},{160,192},{192,224},{224... | collective-permute-start | bytes 1105928 | tf_op jit(solution)/shard_map/ppermute | solution.py:21
  68.5 15.8 %collective-permute-start.25 = (bf16[200,1536]{1,0:T(8,128)(2,1)}, bf16[200,1536]{1,0:T(8,128)(2,1)S(1)}, u32[]{:S(2)}, u32[]{:S(2)}) collective-permute-start(bf16[200,1536]{1,0:T(8,128)(2,1)} %collective-permute-done.19.refs_6_), channel_id=1, source_target_pairs={{0,24},{8,0},{16,8},{24,16},{1,25},{9,1},{17,9},{25,17},{2,26},{10... | collective-permute-start | bytes 1843208 | tf_op jit(solution)/shard_map/ppermute | solution.py:21
  68.9 12.0 %collective-permute-start.24 = (bf16[120,1536]{1,0:T(8,128)(2,1)}, bf16[120,1536]{1,0:T(8,128)(2,1)S(1)}, u32[]{:S(2)}, u32[]{:S(2)}) collective-permute-start(bf16[120,1536]{1,0:T(8,128)(2,1)} %collective-permute-done.9.refs_1_), channel_id=1, source_target_pairs={{0,8},{8,16},{16,24},{24,0},{1,9},{9,17},{17,25},{25,1},{2,10},{10... | collective-permute-start | bytes 1105928 | tf_op jit(solution)/shard_map/ppermute | solution.py:21
  101.2 14.1 %collective-permute-start.27 = (f32[4,128]{1,0:T(4,128)S(1)}, f32[4,128]{1,0:T(4,128)S(1)}, u32[]{:S(2)}, u32[]{:S(2)}) collective-permute-start(f32[4,128]{1,0:T(4,128)S(1)} %log_add_fusion.2), channel_id=1, source_target_pairs={{0,2},{2,4},{4,6},{6,0},{1,3},{3,5},{5,7},{7,1},{8,10},{10,12},{12... | collective-permute-start | bytes 6152 | tf_op jit(solution)/shard_map/ppermute | solution.py:21
  103.6 11.7 %collective-permute-start.28 = (f32[4,128]{1,0:T(4,128)S(1)}, f32[4,128]{1,0:T(4,128)S(1)}, u32[]{:S(2)}, u32[]{:S(2)}) collective-permute-start(f32[4,128]{1,0:T(4,128)S(1)} %log_add_fusion.2), channel_id=1, source_target_pairs={{0,6},{2,0},{4,2},{6,4},{1,7},{3,1},{5,3},{7,5},{8,14},{10,8},{12,... | collective-permute-start | bytes 6152 | tf_op jit(solution)/shard_map/ppermute | solution.py:21
  104.6 10.7 %collective-permute-start.29 = (f32[4,128]{1,0:T(4,128)S(1)}, f32[4,128]{1,0:T(4,128)S(1)}, u32[]{:S(2)}, u32[]{:S(2)}) collective-permute-start(f32[4,128]{1,0:T(4,128)S(1)} %log_add_fusion.2), channel_id=1, source_target_pairs={{0,4},{2,6},{4,0},{6,2},{1,5},{3,7},{5,1},{7,3},{8,12},{10,14},{12... | collective-permute-start | bytes 6152 | tf_op jit(solution)/shard_map/ppermute | solution.py:21
  107.8 19.0 %all-to-all-start.1 = ((f32[32,16,128]{2,1,0:T(8,128)}), f32[32,16,128]{2,1,0:T(8,128)S(1)}, u32[]{:S(2)}, u32[]{:S(2)}) async-start(f32[32,16,128]{2,1,0:T(8,128)} %broadcast_in_dim.8), calls=%async_computation.1 | async-start | bytes 524288 | tf_op jit(solution)/shard_map/all_to_all | solution.py:368
  (24 other events, 131.1 us)
